TPU v7x, 512 devices: a whole 4x4x16 slice. The times are simulated.
512 devices in a mesh: space: 128 (over y, z, core), chan: 4 (over x).
Axes of the slice: x: 4, y: 4, z: 16, core: 2. Of those that a mesh axis runs over, the one named last changes fastest.
Arguments:
- features: float32 [16384, 512], P('space', 'chan'), may hold values from -6 to 6
- weights: float32 [27, 512, 512], P(None, 'space', 'chan'), may hold values from -0.0546875 to 0.0546875
- cotangent: float32 [16384, 512], P('space', 'chan'), may hold values from -6 to 6
- rule_src: int32 [3456, 128], P('space'), may hold values from 0 to 383
- rule_dst: int32 [3456, 128], P('space'), may hold values from 0 to 127, as said below
- block_count: int32 [3456], P('space'), may hold values from 32 to 128, as said below
- send_rows: int32 [16384, 2], P('space'), may hold values from 0 to 127
Outputs:
- conv_out: float32 [16384, 512], P('space', 'chan')
- grad_features: float32 [16384, 512], P('space', 'chan')
Inputs may be any that keep to these rules, and one draw needn't show every extreme that they name: `rule_dst`: for every device and offset, the 1 block hold each of the device's local voxel indices exactly once. `block_count`: every device has at least one full block; rows at or past the count are padding whose indices must be ignored.
All inputs are finite; a program needn't handle non-finite values.
Results may differ from a plain program's by a relative error of at most 0.0003.
Values sent between devices are 32-bit elements; how exact they have to be, the bound alone decides.
No kernel may reach another device: no remote copies, remote signals or barrier semaphores. Data moves between devices by JAX's collectives and lax.ppermute only.
A program may use at most 64 MiB of HBM per device.

v0:
```python
import jax
import jax.numpy as jnp
from jax import lax
from jax.sharding import PartitionSpec as P


def backward_rows(grad_rows, kernel_back, sources, targets, live_rows, table_rows):
    offsets = kernel_back.shape[0]

    def backward_step(offset, running):
        picked = grad_rows[targets[offset]]
        product = jnp.dot(
            picked,
            kernel_back[offset].T,
            precision=lax.Precision.HIGHEST,
            preferred_element_type=jnp.float32,
        )
        return running.at[sources[offset]].add(product * live_rows[offset][:, None])

    start_table = jnp.zeros((table_rows, kernel_back.shape[1]), jnp.float32)
    return lax.fori_loop(0, offsets, backward_step, start_table)


def on_device(features, weights, cotangent, rule_src, rule_dst, block_count, send_rows):
    local_count = features.shape[0]
    quarter = features.shape[1]
    peer_count = lax.axis_size("space")
    per_peer = send_rows.shape[1]
    block_rows = rule_src.shape[1]
    offsets = weights.shape[0]
    live_rows = (jnp.arange(block_rows, dtype=jnp.int32)[None, :] < block_count[:, None]).astype(
        jnp.float32
    )
    send_flat = send_rows.reshape(-1)
    outgoing = features[send_flat].reshape(peer_count, per_peer, quarter)
    incoming = lax.all_to_all(outgoing, "space", split_axis=0, concat_axis=0, tiled=True)
    joined = jnp.concatenate([features, incoming.reshape(peer_count * per_peer, quarter)], 0)
    extended = lax.all_gather(joined, "chan", axis=1, tiled=True)
    weight_full = lax.all_gather(weights, "space", axis=1, tiled=True)

    def forward_step(offset, running):
        picked = extended[rule_src[offset]]
        product = jnp.dot(
            picked,
            weight_full[offset],
            precision=lax.Precision.HIGHEST,
            preferred_element_type=jnp.float32,
        )
        return running.at[rule_dst[offset]].add(product * live_rows[offset][:, None])

    conv_out = lax.fori_loop(
        0, offsets, forward_step, jnp.zeros((local_count, quarter), jnp.float32)
    )
    table_rows = extended.shape[0]
    weight_back = lax.all_gather(weights, "space", axis=1, tiled=True)
    grad_extended = backward_rows(cotangent, weight_back, rule_src, rule_dst, live_rows, table_rows)
    grad_parts = lax.psum_scatter(grad_extended, "chan", scatter_dimension=1, tiled=True)
    returned = lax.all_to_all(
        grad_parts[local_count:].reshape(peer_count, per_peer, quarter),
        "space",
        split_axis=0,
        concat_axis=0,
        tiled=True,
    )
    grad_features = grad_parts[:local_count].at[send_flat].add(returned.reshape(-1, quarter))
    return (conv_out, grad_features)


def solution(mesh):
    placed = (
        P("space", "chan"),
        P(None, "space", "chan"),
        P("space", "chan"),
        P("space", None),
        P("space", None),
        P("space"),
        P("space", None),
    )
    return jax.shard_map(
        on_device,
        mesh=mesh,
        in_specs=placed,
        out_specs=(P("space", "chan"), P("space", "chan")),
        check_vma=False,
    )
```

profile of v0, /device:TPU:1, one launch (start us, length us, event | category | flops | bytes accessed | tf_op | source)
XLA Modules:
  0.0 468.0 jit_solution(12968796980760491436)
XLA Ops:
  9.5 155.0 %all-gather.2.cloned.1.call-done = f32[27,512,128]{2,0,1:T(8,128)} async-done(((f32[27,4,128]{2,0,1:T(8,128)}), f32[27,512,128]{2,0,1:T(8,128)}) %all-gather.2.cloned.1.call-update) | async-done | bytes 7077904 | tf_op jit(solution)/shard_map/all_gather | solution.py:39
  164.5 10.4 %copy.12 = f32[27,512,128]{2,1,0:T(8,128)} copy(f32[27,512,128]{2,0,1:T(8,128)} %all-gather.2.cloned.1.call-done) | data formatting | bytes 14155776 | tf_op jit(solution)/shard_map/while | solution.py:51
  175.0 118.8 %while.27 = (s32[]{:T(128)}, f32[384,512]{1,0:T(8,128)S(1)}, s32[27,128]{1,0:T(8,128)}, s32[27,128]{1,0:T(8,128)}, f32[128,128]{1,0:T(8,128)S(1)}, /*index=5*/f3...) while((s32[]{:T(128)}, f32[384,512]{1,0:T(8,128)S(1)}, s32[27,128]{1,0:T(8,128)}, s32[27,128]{1,0:T(8,128)}, ...), condition=%wide.region_5.0_spmd, body=%wide.region_3.0_spmd.sunk | while | flops 100796160 | bytes 1517149 | solution.py:21
  177.8 1.7 scatter_fusion.1
  182.2 1.7 scatter_fusion.1
  186.6 1.7 scatter_fusion.1
  195.4 1.7 scatter_fusion.1
  208.6 1.7 scatter_fusion.1
  217.4 1.7 scatter_fusion.1
  221.8 1.7 scatter_fusion.1
  230.6 1.7 scatter_fusion.1
  235.0 1.7 scatter_fusion.1
  239.4 1.7 scatter_fusion.1
  243.8 1.7 scatter_fusion.1
  248.2 1.7 scatter_fusion.1
  252.6 1.7 scatter_fusion.1
  257.0 1.7 scatter_fusion.1
  261.4 1.7 scatter_fusion.1
  265.8 1.7 scatter_fusion.1
  295.8 27.1 %all_to_all.10 = f32[128,2,128]{2,1,0:T(2,128)S(1)} all-to-all(f32[128,2,128]{2,1,0:T(2,128)S(1)} %bitcast.71), channel_id=1, replica_groups=mesh['space'=128,'chan'=4] {'space'}, dimensions={0} | all-to-all | bytes 262144 | tf_op jit(solution)/shard_map/all_to_all | solution.py:36
  322.8 12.0 %all_gather.7 = f32[384,512]{1,0:T(8,128)S(1)} all-gather(f32[384,128]{1,0:T(8,128)S(1)} %pad_maximum_fusion), channel_id=1, replica_groups=mesh['space'=128,'chan'=4] {'chan'}, dimensions={1}, use_global_device_ids=true | all-gather | bytes 983040 | tf_op jit(solution)/shard_map/all_gather | solution.py:38
  336.4 9.5 %all-to-all-start.1 = ((f32[128,2,128]{2,1,0:T(2,128)}), f32[128,2,128]{2,1,0:T(2,128)S(1)}, u32[]{:S(2)}, u32[]{:S(2)}) async-start(f32[128,2,128]{2,1,0:T(2,128)} %bitcast.15), calls=%async_computation.2 | async-start | bytes 262144 | tf_op jit(solution)/shard_map/all_to_all | solution.py:58
  345.9 112.6 %while.26 = (s32[]{:T(128)}, f32[128,128]{1,0:T(8,128)S(1)}, s32[27,128]{1,0:T(8,128)}, s32[27,128]{1,0:T(8,128)}, f32[384,512]{1,0:T(8,128)S(1)}, /*index=5*/f3...) while((s32[]{:T(128)}, f32[128,128]{1,0:T(8,128)S(1)}, s32[27,128]{1,0:T(8,128)}, s32[27,128]{1,0:T(8,128)}, ...), condition=%wide.region_2.0_spmd, body=%wide.region_0.0_spmd.sunk | while | flops 100697856 | bytes 1320541 | solution.py:51
  458.6 2.0 scatter_fusion.2
  (339 shorter events, 209.3 us)
Async XLA Ops:
  7.2 157.3 %all-gather.2.cloned.1.call-start = ((), (), s32[]{:S(2)}) async-start(), calls=%async_computation.3 | async-start | bytes 8454144 | tf_op jit(solution)/shard_map/all_gather | solution.py:39
  8.7 326.1 %reduce-scatter.2.cloned.1.call-start = ((), (), s32[]{:S(2)}) async-start(), calls=%async_computation.4 | async-start | bytes 983040 | tf_op jit(solution)/shard_map/reduce_scatter | solution.py:57
  9.5 165.5 %copy-start.2 = (f32[128,128]{1,0:T(8,128)S(1)}, f32[128,128]{1,0:T(8,128)}, u32[]{:S(2)}) copy-start(f32[128,128]{1,0:T(8,128)} %param.13) | copy-start | bytes 196612
  175.0 119.7 %copy-start.5 = (s32[128,2]{0,1:T(2,128)S(1)}, s32[128,2]{0,1:T(2,128)}, u32[]{:S(2)}) copy-start(s32[128,2]{0,1:T(2,128)} %param.17) | copy-start | bytes 3076
  175.0 120.0 %copy-start.3 = (f32[128,128]{1,0:T(8,128)S(1)}, f32[128,128]{1,0:T(8,128)}, u32[]{:S(2)}) copy-start(f32[128,128]{1,0:T(8,128)} %param.11) | copy-start | bytes 196612
  293.8 0.9 copy-start
  336.4 122.1 %all-to-all-start.1 = ((f32[128,2,128]{2,1,0:T(2,128)}), f32[128,2,128]{2,1,0:T(2,128)S(1)}, u32[]{:S(2)}, u32[]{:S(2)}) async-start(f32[128,2,128]{2,1,0:T(2,128)} %bitcast.15), calls=%async_computation.2 | async-start | bytes 262144 | tf_op jit(solution)/shard_map/all_to_all | solution.py:58
  345.9 112.6 %slice-start = ((f32[384,128]{1,0:T(8,128)}), f32[128,128]{1,0:T(8,128)S(1)}, s32[]{:S(2)}) async-start(f32[384,128]{1,0:T(8,128)} %reduce-scatter.2.cloned.1.call-done), calls=%async_computation.5 | async-start | bytes 131072 | tf_op jit(solution)/shard_map/slice | solution.py:65
  458.5 2.0 copy-start.1
  460.5 0.6 copy-start.4
Sparse Core Ops, SparseCore 0:
  11.7 152.7 all-gather.1
  294.9 23.6 reduce-scatter.1
where the time goes:
time: 472 us; the launch traced here: 468 us
  waiting for transfers between devices  155 us (33%)
  other arithmetic  122 us (26%)
  matrix products  72.1 us (15%)
  local copies, waits for them, and re-layouts  54.3 us (12%)
  blocking collectives  39 us (8%)
  between operations  14.2 us (3%)
  starting transfers between devices  9.57 us (2%)
    all_gather x1, waiting for transfers between devices, on_device(): weight_full = lax.all_gather(weights, 'space', axis=1, tiled=True)  155 us
    scatter-add x27, other arithmetic, backward_step(): return running.at[sources[offset]].add(product * live_rows[offset][:, None])  44.6 us
    dot_general x27, matrix products, forward_step(): jnp.dot(picked, weight_full[offset], precision=lax.Precision.HIGHEST, pre...  36.2 us
    dot_general x27, matrix products, backward_step(): jnp.dot(picked, kernel_back[offset].T, precision=lax.Precision.HIGHEST, p...  35.9 us
    scatter-add x27, other arithmetic, forward_step(): running.at[rule_dst[offset]].add(product * live_rows[offset][:, None])  35 us
    all_to_all x1, blocking collectives, on_device(): lax.all_to_all(outgoing, 'space', split_axis=0, concat_axis=0, tiled=True)  27.1 us
    gather x27, local copies, waits for them, and re-layouts, forward_step(): picked = extended[rule_src[offset]]  20.4 us
    select_n x27, other arithmetic, backward_step(): return running.at[sources[offset]].add(product * live_rows[offset][:, None])  19.4 us
  transfers between devices with their start and end apart: 3, of which 1 were waited for; matrix products, arithmetic and copies ran while one was open for 24% of the time, Pallas kernels for 0%

commit v1 on v0

v1 whole, which is shorter than its diff:
```python
import jax
import jax.numpy as jnp
from jax import lax
from jax.experimental import pallas as pl
from jax.experimental.pallas import tpu as pltpu
from jax.sharding import PartitionSpec as P

F32 = jnp.float32
BF16 = jnp.bfloat16
NY = 4
CORES = 2
CHUNKS = 3
SMALL, LARGE = 16, 63


def iota(shape, dim):
    return lax.broadcasted_iota(jnp.int32, shape, dim)


def split2(x):
    high = x.astype(BF16)
    return high, (x - high.astype(F32)).astype(BF16)


def split3(x):
    high = x.astype(BF16)
    rest = x - high.astype(F32)
    middle = rest.astype(BF16)
    return high, middle, (rest - middle.astype(F32)).astype(BF16)


def dot(a, b):
    return jnp.dot(a, b, preferred_element_type=F32)


def as_onehot(mask):
    return jnp.where(mask, 1.0, 0.0).astype(BF16)


def pick_left(onehot, x):
    a, b, c = split3(x)
    return (dot(onehot, a) + dot(onehot, b)) + dot(onehot, c)


def pick_right(x, onehot):
    a, b, c = split3(x)
    return (dot(a, onehot) + dot(b, onehot)) + dot(c, onehot)


def to_inner(n):
    row = iota((n, n), 0)
    place = ((row >> 2) & 1) * 64 + (row >> 3) * 4 + (row & 3)
    return as_onehot(iota((n, n), 1) == place)


def from_inner(n):
    row = iota((n, n), 0)
    place = ((row >> 2) & 15) * 8 + (row >> 6) * 4 + (row & 3)
    return as_onehot(iota((n, n), 1) == place)


FEATURES, SOURCES, TARGETS, SENDS, SHARED = 128, 256, 288, 320, 328


def onehot_rows(line, rows):
    return as_onehot(line.astype(jnp.int32) == iota((rows, line.shape[1]), 0))


def started(pairs, sems):
    copies = [pltpu.make_async_copy(a, b, sems.at[i]) for i, (a, b) in enumerate(pairs)]
    for copy in copies:
        copy.start()
    return copies


def prepare_kernel(
    count_ref, features_in, cot_in, send_in, src_in, dst_in, shared_ref,
    features_ref, send_ref, src_ref, dst_ref, sems,
):
    rows, width = features_ref.shape
    offsets, block = src_ref.shape
    copies = started(
        [
            (features_in, features_ref),
            (send_in, send_ref),
            (src_in, src_ref),
            (dst_in, dst_ref),
            (cot_in, shared_ref.at[pl.ds(0, rows)]),
        ],
        sems,
    )
    for copy in copies:
        copy.wait()
    shared_ref[FEATURES : FEATURES + rows, :] = pick_right(features_ref[...], to_inner(width))
    shared_ref[SOURCES:SHARED, :] = jnp.zeros((SHARED - SOURCES, width), F32)
    for k in range(offsets):
        live = iota((1, block), 1) < count_ref[k]
        shared_ref[SOURCES + k : SOURCES + k + 1, :] = jnp.where(live, src_ref[k : k + 1, :], -1).astype(F32)
    shared_ref[TARGETS : TARGETS + offsets, :] = dst_ref[...].astype(F32)
    shared_ref[SENDS : SENDS + send_ref.shape[0], :] = send_ref[...].astype(F32)


def outgoing_kernel(core_ref, shared_ref, outgoing_ref, cot_ref, sends_ref, picked_ref):
    rows, width = picked_ref.shape
    half = width // CORES
    slots = sends_ref.shape[0] // CORES
    chips = picked_ref.shape[0] // CORES
    for device in range(CORES):
        base = device * SHARED
        cot_ref[device * rows : (device + 1) * rows, :] = shared_ref[base : base + rows, :]
        inner = shared_ref[base + FEATURES : base + FEATURES + rows, :]
        parts = split3(pltpu.roll(inner, half * core_ref[0], axis=1))
        for slot in range(slots):
            line = shared_ref[base + SENDS + slot : base + SENDS + slot + 1, :]
            sends_ref[device * slots + slot : device * slots + slot + 1, :] = line
            onehot = onehot_rows(line, rows)
            a, b, c = (
                lax.dot_general(onehot, part, (((0,), (0,)), ((), ())), preferred_element_type=F32)
                for part in parts
            )
            picked_ref[...] = (a + b) + c
            both = [picked_ref[pl.ds(d, chips, stride=CORES), :][:, :half] for d in range(CORES)]
            outgoing_ref[pl.ds(device * slots + slot, chips, stride=CORES * slots), :] = jnp.concatenate(
                both, axis=1
            )


def regroup_kernel(gathered_ref, grouped_ref):
    offsets, inner, _ = grouped_ref.shape
    depth = gathered_ref.shape[1]
    for k in range(offsets):
        for z in range(inner // depth):
            grouped_ref[k, z * depth : (z + 1) * depth, :] = gathered_ref[z * offsets + k]


def pairs_of(shared_ref, device, k, local, rows):
    start = device * SHARED + k
    src = shared_ref[start + SOURCES : start + SOURCES + 1, :]
    dst = shared_ref[start + TARGETS : start + TARGETS + 1, :]
    mine = dst == iota((local, dst.shape[1]), 0).astype(F32)
    source = jnp.sum(jnp.where(mine, src + 1.0, 0.0), axis=1, keepdims=True)
    return as_onehot(iota((local, rows), 1) == source.astype(jnp.int32) - 1)


def kernel_rows(pieces):
    wide = jnp.concatenate(pieces, axis=2)
    return wide.reshape(wide.shape[0] * wide.shape[1], wide.shape[2])


def core_kernel(order_ref, *refs):
    shared_in, incoming_in = refs[:2]
    cot_in = refs[2 : NY + 2]
    piece_in = refs[NY + 2 : 2 * NY + 2]
    refs = refs[2 * NY + 2 :]
    halo_out, local_ref, other_ref, *part_outs = refs[: NY + 3]
    shared_ref, incoming_ref, cot_ref, pieces_ref, turned_ref, table_ref, total_ref, halo_ref = refs[
        NY + 3 : -4
    ]
    first_sems, cot_sems, piece_sems, out_sems = refs[-4:]
    rows, width = part_outs[0].shape
    both_rows = CORES * rows
    table_rows = table_ref.shape[0]
    offsets = pieces_ref.shape[1]
    half = pieces_ref.shape[2]
    step = offsets // CHUNKS
    core = order_ref[NY]

    def piece_copy(chunk, n):
        span = pl.ds(chunk * step, step)
        return pltpu.make_async_copy(piece_in[n].at[span], pieces_ref.at[n, span], piece_sems.at[chunk, n])

    first = [
        pltpu.make_async_copy(shared_in, shared_ref, first_sems.at[0]),
        pltpu.make_async_copy(incoming_in, incoming_ref, first_sems.at[1]),
    ]
    cots = [
        pltpu.make_async_copy(cot_in[m], cot_ref.at[m], cot_sems.at[m])
        for m in range(NY)
    ]
    for copy in first + cots:
        copy.start()
    for chunk in range(CHUNKS):
        for n in range(NY):
            piece_copy(chunk, n).start()
    for copy in first + cots:
        copy.wait()
    for n in range(NY):
        high, low = split2(cot_ref[order_ref[NY + 1 + n]].T)
        turned_ref[n * width : (n + 1) * width, :both_rows] = high
        turned_ref[n * width : (n + 1) * width, both_rows:] = low
    local = [
        pltpu.roll(
            shared_ref[d * SHARED + FEATURES : d * SHARED + FEATURES + rows, :], half * core, axis=1
        )[:, :half]
        for d in range(CORES)
    ]
    table = jnp.concatenate([jnp.concatenate(local, axis=1), incoming_ref[...]], axis=0)
    high, low = split2(table)
    table_ref[:, :width] = high
    table_ref[:, width:] = low

    grads = [None] * CORES
    total = None
    for chunk in range(CHUNKS):
        pairs = [
            jnp.concatenate(
                [pairs_of(shared_ref, d, chunk * step + k, rows, table_rows) for k in range(step)], axis=0
            )
            for d in range(CORES)
        ]
        picked = []
        for device in range(CORES):
            both = dot(pairs[device], table_ref[...]).astype(BF16)
            for start in (device * half, width + device * half):
                picked.append(
                    jnp.concatenate(
                        [both[k * rows : (k + 1) * rows, start : start + half] for k in range(step)],
                        axis=1,
                    )
                )
        highs = jnp.concatenate([picked[0], picked[2]], axis=0)
        lows = jnp.concatenate([picked[1], picked[3]], axis=0)
        for n in range(NY):
            piece_copy(chunk, n).wait()
        span = slice(chunk * step, (chunk + 1) * step)
        high, low = split2(kernel_rows([pieces_ref[n, span] for n in range(NY)]))
        product = dot(highs, high) + dot(lows, high) + dot(highs, low)
        total = product if chunk == 0 else total + product
        wide = dot(high, turned_ref[...])
        product = wide[:, :both_rows] + wide[:, both_rows:] + dot(low, turned_ref[:, :both_rows])
        product = product.reshape(step, half, both_rows)
        for device in range(CORES):
            side = jnp.concatenate(
                [product[k][:, device * rows : (device + 1) * rows] for k in range(step)], axis=1
            )
            both = dot(jnp.concatenate(split2(side), axis=0), pairs[device])
            both = both[:half] + both[half:]
            grads[device] = both if chunk == 0 else grads[device] + both
    table = jnp.concatenate(grads, axis=0).T
    halo_ref[...] = table[rows:, :]
    outs = [pltpu.make_async_copy(halo_ref, halo_out, out_sems.at[NY])]
    outs[0].start()
    local_ref[...] = table[:rows, :]
    for n in range(NY):
        for device in range(CORES):
            part = total[device * rows : (device + 1) * rows, n * width : (n + 1) * width]
            total_ref[device, n] = part
    for s in range(NY):
        outs.append(
            pltpu.make_async_copy(
                total_ref.at[core, order_ref[2 * NY + 1 + s]], part_outs[s], out_sems.at[s]
            )
        )
        outs[-1].start()
        other_ref[s * rows : (s + 1) * rows, :] = total_ref[1 - core, order_ref[2 * NY + 1 + s]]
    for copy in outs:
        copy.wait()


def finish_kernel(core_ref, local_ref, returned_ref, sends_ref, own_ref, other_ref, grads_ref, full_ref):
    rows, width = own_ref.shape
    half = width // CORES
    slots = sends_ref.shape[0] // CORES
    chips = sends_ref.shape[1] // CORES
    spread = from_inner(width)
    spread = jnp.where(core_ref[0] == 0, spread[:half, :], spread[half:, :])
    for device in range(CORES):
        total = local_ref[:, device * half : (device + 1) * half]
        for slot in range(slots):
            line = device * slots + slot
            part = returned_ref[pl.ds(line, chips, stride=CORES * slots), :]
            for d in range(CORES):
                grads_ref[pl.ds(d, chips, stride=CORES), :half] = part[:, d * half : (d + 1) * half]
            onehot = onehot_rows(sends_ref[line : line + 1, :], rows)
            total = total + pick_left(onehot, grads_ref[:, :half])
        full_ref[device] = pick_right(total, spread)
    own_ref[...] = full_ref[core_ref[0]]
    other_ref[...] = full_ref[1 - core_ref[0]]


VMEM = pl.BlockSpec(memory_space=pltpu.VMEM)
HBM = pl.BlockSpec(memory_space=pl.ANY)
SMEM = pl.BlockSpec(memory_space=pltpu.SMEM)


def params(mebibytes):
    return pltpu.CompilerParams(vmem_limit_bytes=mebibytes * 1024 * 1024)


def whole(kernel, outs, args, in_specs=None, out_specs=None, scratch=(), mebibytes=16):
    return pl.pallas_call(
        kernel,
        out_shape=tuple(jax.ShapeDtypeStruct(s, t) for s, t in outs),
        in_specs=in_specs or [VMEM] * len(args),
        out_specs=tuple(out_specs or [VMEM] * len(outs)),
        scratch_shapes=list(scratch),
        compiler_params=params(mebibytes),
    )(*args)


def on_device(features, weights, cotangent, rule_src, rule_dst, block_count, send_rows):
    space = lax.axis_size("space")
    chan = lax.axis_size("chan")
    nz = space // (NY * CORES)
    rows, width = features.shape
    offsets = weights.shape[0]
    peers, slots = send_rows.shape
    halo_rows = peers * slots
    table_rows = rows + halo_rows
    half = width // CORES

    def place(y, z, core):
        return ((y % NY) * nz + z) * CORES + core

    where = [(y, z, core) for y in range(NY) for z in range(nz) for core in range(CORES)]
    z_groups = [[place(b, z, c) for z in range(nz)] for b in range(NY) for c in range(CORES)]
    core_groups = [[place(b, z, c) for b in range(NY) for z in range(nz)] for c in range(CORES)]
    chip_groups = [[place(b, z, c) for c in range(CORES)] for b in range(NY) for z in range(nz)]

    def along_y(x, step):
        return lax.ppermute(x, "space", [(place(y, z, c), place(y - step, z, c)) for y, z, c in where])

    def along_x(x, step):
        return lax.ppermute(x, "chan", [(a, (a - step) % chan) for a in range(chan)])

    def of_chip(x):
        return lax.all_gather(x, "space", axis=0, tiled=False, axis_index_groups=chip_groups)

    y = lax.axis_index("space") // (nz * CORES)
    core = lax.axis_index("space") % CORES
    turn = jnp.arange(NY, dtype=jnp.int32)
    x = lax.axis_index("chan")
    order = [(y + turn) % NY, core[None], (y + turn - x) % NY, (x + turn - y) % NY]
    order = jnp.concatenate(order).astype(jnp.int32)
    core = core[None]

    swapped = lax.ppermute(
        weights,
        ("space", "chan"),
        [(place(b, z, c) * chan + a, place(a, z, c) * chan + b) for b, z, c in where for a in range(chan)],
    )
    (shared,) = whole(
        prepare_kernel,
        [((SHARED, width), F32)],
        (block_count, features, cotangent, send_rows.T, rule_src, rule_dst),
        in_specs=[SMEM] + [HBM] * 5,
        scratch=[
            pltpu.VMEM((rows, width), F32),
            pltpu.VMEM((slots, peers), jnp.int32),
            pltpu.VMEM(rule_src.shape, jnp.int32),
            pltpu.VMEM(rule_dst.shape, jnp.int32),
            pltpu.SemaphoreType.DMA((5,)),
        ],
        mebibytes=SMALL,
    )
    shared = of_chip(shared).reshape(CORES * SHARED, width)
    swapped, shared = lax.optimization_barrier((swapped, shared))
    gathered = lax.all_gather(swapped, "space", axis=0, tiled=True, axis_index_groups=z_groups)
    (own,) = whole(regroup_kernel, [((offsets, 4 * nz, width), F32)], (gathered,), mebibytes=SMALL)
    shared, own = lax.optimization_barrier((shared, own))
    pieces = [own] + [along_y(own, s) for s in (1, 2, 3)]
    outgoing, cots, sends = whole(
        outgoing_kernel,
        [((halo_rows, width), F32), ((CORES * rows, width), F32), ((CORES * slots, peers), F32)],
        (core, shared),
        in_specs=[SMEM, VMEM],
        scratch=[pltpu.VMEM((peers, width), F32)],
        mebibytes=SMALL,
    )
    cots = [cots] + [along_x(cots, s) for s in (1, 2, 3)]

    def exchange(x):
        x = x.reshape(peers // CORES, CORES * slots, width)
        x = lax.all_to_all(
            x, "space", split_axis=0, concat_axis=0, tiled=True, axis_index_groups=core_groups
        )
        return x.reshape(halo_rows, width)

    incoming = exchange(outgoing)
    halo_grad, local_grad, other_parts, *parts = whole(
        core_kernel,
        [((halo_rows, width), F32), ((rows, width), F32), ((NY * rows, width), F32)]
        + [((rows, width), F32)] * NY,
        (order, shared, incoming, *cots, *pieces),
        in_specs=[SMEM] + [HBM] * (2 * NY + 2),
        out_specs=[HBM] + [VMEM] * 2 + [HBM] * NY,
        scratch=[
            pltpu.VMEM(shared.shape, F32),
            pltpu.VMEM(incoming.shape, F32),
            pltpu.VMEM((NY, CORES * rows, width), F32),
            pltpu.VMEM((NY, *own.shape), F32),
            pltpu.VMEM((NY * width, 2 * CORES * rows), BF16),
            pltpu.VMEM((table_rows, 2 * width), BF16),
            pltpu.VMEM((CORES, NY, rows, width), F32),
            pltpu.VMEM((halo_rows, width), F32),
            pltpu.SemaphoreType.DMA((2,)),
            pltpu.SemaphoreType.DMA((NY,)),
            pltpu.SemaphoreType.DMA((CHUNKS, NY)),
            pltpu.SemaphoreType.DMA((NY + 1,)),
        ],
        mebibytes=LARGE,
    )
    returned = exchange(halo_grad)
    other_parts = lax.dynamic_index_in_dim(of_chip(other_parts), 1 - core[0], 0, False)
    parts = [p + other_parts[s * rows : (s + 1) * rows] for s, p in enumerate(parts)]
    conv_out = parts[0] + along_x(parts[3], 1) + along_x(parts[2], 2) + along_x(parts[1], 3)
    own_grad, other_grad = whole(
        finish_kernel,
        [((rows, width), F32)] * 2,
        (core, local_grad, returned, sends),
        in_specs=[SMEM] + [VMEM] * 3,
        scratch=[pltpu.VMEM((peers, width), F32), pltpu.VMEM((CORES, rows, width), F32)],
        mebibytes=SMALL,
    )
    other_grad = lax.dynamic_index_in_dim(of_chip(other_grad), 1 - core[0], 0, False)
    return (conv_out, own_grad + other_grad)


def solution(mesh):
    placed = (
        P("space", "chan"),
        P(None, "space", "chan"),
        P("space", "chan"),
        P("space", None),
        P("space", None),
        P("space"),
        P("space", None),
    )
    return jax.shard_map(
        on_device,
        mesh=mesh,
        in_specs=placed,
        out_specs=(P("space", "chan"), P("space", "chan")),
        check_vma=False,
    )
```

time: 472 us -> 143 us (0.30)
  waiting for transfers between devices: 155 us -> 24.8 us
  other arithmetic: 122 us -> 1.98 us
  matrix products: 72.1 us -> 0 us
  local copies, waits for them, and re-layouts: 54.3 us -> 4.53 us
  starting transfers between devices: 9.57 us -> 47.5 us
  Pallas kernels: 0 us -> 17.6 us
  between operations: 14.2 us -> 0.98 us
  blocking collectives: 39 us -> 44.4 us
    all_gather x1 -> x0, waiting for transfers between devices: 155 us -> none  [on_device(): weight_full = lax.all_gather(weights, 'space', axis=1, tiled=True)]
    scatter-add x55 -> x0, other arithmetic: 81.6 us -> none  [the longest x27 44.6 us: backward_step(): return running.at[sources[offset]].add(product * live_rows[offset][:, None])]
    dot_general x54 -> x0, matrix products: 72.1 us -> none  [the longest x27 36.2 us: forward_step(): jnp.dot(picked, weight_full[offset], precision=lax.Precision.HIGHEST, pre...]
    select_n x55 -> x2, other arithmetic: 38.7 us -> 0.02 us  [the longest x1 0.01 us: on_device(): (x + turn - y) % NY]
    gather x55 -> x0, local copies, waits for them, and re-layouts: 38.6 us -> none  [the longest x27 20.4 us: forward_step(): picked = extended[rule_src[offset]]]
    all_gather x1 -> x4, blocking collectives: 12 us -> 44.4 us  [the longest x1 28.7 us: on_device(): lax.all_gather(swapped, 'space', axis=0, tiled=True, axis_index_groups=z_...]
    ppermute x0 -> x10, starting transfers between devices: none -> 31.7 us  [the longest x6 17.3 us: along_x(): lax.ppermute(x, 'chan', [(a, (a - step) % chan) for a in range(chan)])]
    all_to_all x1 -> x0, blocking collectives: 27.1 us -> none  [on_device(): lax.all_to_all(outgoing, 'space', split_axis=0, concat_axis=0, tiled=True)]
  transfers between devices with their start and end apart: 3 -> 12, of which waited for: 1 -> 5; matrix products, arithmetic and copies ran while one was open for 24% -> 1% of each run, Pallas kernels for 0% -> 1%
where the time goes in v1:
time: 143 us; the launch traced here: 142 us
  starting transfers between devices  47.5 us (33%)
  blocking collectives  44.4 us (31%)
  waiting for transfers between devices  24.8 us (17%)
  Pallas kernels  17.6 us (12%)
  local copies, waits for them, and re-layouts  4.53 us (3%)
  other arithmetic  1.98 us (1%)
    all_gather x1, blocking collectives, on_device(): lax.all_gather(swapped, 'space', axis=0, tiled=True, axis_index_groups=z_...  28.7 us
    pallas_call x5, Pallas kernels, whole(): pl.pallas_call(kernel, out_shape=tuple((jax.ShapeDtypeStruct(s, t) for s,...  17.6 us
    ppermute x6, starting transfers between devices, along_x(): lax.ppermute(x, 'chan', [(a, (a - step) % chan) for a in range(chan)])  17.3 us
    all_to_all x2, starting transfers between devices, exchange(): lax.all_to_all(x, 'space', split_axis=0, concat_axis=0, tiled=True, axis_...  15.8 us
    all_gather x3, blocking collectives, of_chip(): lax.all_gather(x, 'space', axis=0, tiled=False, axis_index_groups=chip_gr...  15.8 us
    all_to_all x2, waiting for transfers between devices, exchange(): lax.all_to_all(x, 'space', split_axis=0, concat_axis=0, tiled=True, axis_...  15.6 us
    ppermute x3, starting transfers between devices, along_y(): lax.ppermute(x, 'space', [(place(y, z, c), place(y - step, z, c)) for y,...  12.8 us
    ppermute x6, waiting for transfers between devices, along_x(): lax.ppermute(x, 'chan', [(a, (a - step) % chan) for a in range(chan)])  9.1 us
  transfers between devices with their start and end apart: 12, of which 5 were waited for; matrix products, arithmetic and copies ran while one was open for 1% of the time, Pallas kernels for 1%

profile of v1, /device:TPU:1, one launch (start us, length us, event | category | flops | bytes accessed | tf_op | source)
XLA Modules:
  0.0 141.8 jit_solution(9428076242827950760)
XLA Ops:
  0.7 1.6 %collective-permute-start = (f32[27,4,128]{2,1,0:T(4,128)}, f32[27,4,128]{2,1,0:T(4,128)S(1)}, u32[]{:S(2)}, u32[]{:S(2)}) collective-permute-start(f32[27,4,128]{2,1,0:T(4,128)} %param.8), channel_id=1, source_target_pairs={{0,0},{1,128},{2,256},{3,384},{4,4},{5,132},{6,260},{7,388},{8,8},... | collective-permute-start | bytes 165896 | tf_op jit(solution)/shard_map/ppermute | solution.py:337
  5.4 1.0 shard_map.86
  6.4 8.6 %all-gather.shared_ref.refs_0_ = f32[656,128]{1,0:T(8,128)S(1)} all-gather(f32[328,128]{1,0:T(8,128)S(1)} %shard_map.86), channel_id=2, replica_groups={{0,4},{8,12},{16,20},{24,28},{32,36},{40,44},{48,52},{56,60},{64,68},{7..., dimensions={0}, use_global_device_ids=true | all-gather | bytes 503808 | tf_op jit(solution)/shard_map/all_gather | solution.py:327
  14.9 28.7 %all_gather.23.gathered_ref = f32[432,4,128]{2,1,0:T(4,128)S(1)} all-gather(f32[27,4,128]{2,1,0:T(4,128)S(1)} %collective-permute-done), channel_id=1, replica_groups={{0,8,16,24,32,40,48,56,64,72,80,88,96,104,112,120},{4,12,20,28,36,44,52..., dimensions={0}, use_global_device_ids=true | all-gather | bytes 940032 | tf_op jit(solution)/shard_map/all_gather | solution.py:358
  43.8 7.5 %collective-permute-start.4 = (f32[27,64,128]{2,1,0:T(8,128)S(1)}, f32[27,64,128]{2,1,0:T(8,128)S(1)}, u32[]{:S(2)}, u32[]{:S(2)}) collective-permute-start(f32[27,64,128]{2,1,0:T(8,128)S(1)} %shard_map.87.refs_6_), channel_id=1, source_target_pairs={{0,384},{4,388},{8,392},{12,396},{16,400},{20,404},{24,408},{28,41... | collective-permute-start | bytes 2654216 | tf_op jit(solution)/shard_map/ppermute | solution.py:321
  51.3 2.5 %collective-permute-start.5 = (f32[27,64,128]{2,1,0:T(8,128)S(1)}, f32[27,64,128]{2,1,0:T(8,128)S(1)}, u32[]{:S(2)}, u32[]{:S(2)}) collective-permute-start(f32[27,64,128]{2,1,0:T(8,128)S(1)} %shard_map.87.refs_6_), channel_id=1, source_target_pairs={{0,256},{4,260},{8,264},{12,268},{16,272},{20,276},{24,280},{28,28... | collective-permute-start | bytes 2654216 | tf_op jit(solution)/shard_map/ppermute | solution.py:321
  53.8 2.8 %collective-permute-start.6 = (f32[27,64,128]{2,1,0:T(8,128)S(1)}, f32[27,64,128]{2,1,0:T(8,128)}, u32[]{:S(2)}, u32[]{:S(2)}) collective-permute-start(f32[27,64,128]{2,1,0:T(8,128)S(1)} %shard_map.87.refs_6_), channel_id=1, source_target_pairs={{0,128},{4,132},{8,136},{12,140},{16,144},{20,148},{24,152},{28,15... | collective-permute-start | bytes 2654216 | tf_op jit(solution)/shard_map/ppermute | solution.py:321
  56.6 1.1 shard_map.88
  57.6 8.5 %all-to-all-start = ((f32[64,4,128]{2,1,0:T(4,128)}), f32[64,4,128]{2,1,0:T(4,128)S(1)}, u32[]{:S(2)}, u32[]{:S(2)}) async-start(f32[64,4,128]{2,1,0:T(4,128)} %bitcast.2), calls=%async_computation | async-start | bytes 262144 | tf_op jit(solution)/shard_map/all_to_all | solution.py:374
  66.1 4.9 %collective-permute-start.1 = (f32[256,128]{1,0:T(8,128)S(1)}, f32[256,128]{1,0:T(8,128)S(1)}, u32[]{:S(2)}, u32[]{:S(2)}) collective-permute-start(f32[256,128]{1,0:T(8,128)S(1)} %get-tuple-element.22.refs_2_), channel_id=1, source_target_pairs={{0,3},{1,0},{2,1},{3,2},{4,7},{5,4},{6,5},{7,6},{8,11},{9,8},{10,9... | collective-permute-start | bytes 393224 | tf_op jit(solution)/shard_map/ppermute | solution.py:324
  71.0 2.0 %collective-permute-start.2 = (f32[256,128]{1,0:T(8,128)S(1)}, f32[256,128]{1,0:T(8,128)S(1)}, u32[]{:S(2)}, u32[]{:S(2)}) collective-permute-start(f32[256,128]{1,0:T(8,128)S(1)} %get-tuple-element.22.refs_2_), channel_id=1, source_target_pairs={{0,2},{1,3},{2,0},{3,1},{4,6},{5,7},{6,4},{7,5},{8,10},{9,11},{10,... | collective-permute-start | bytes 393224 | tf_op jit(solution)/shard_map/ppermute | solution.py:324
  73.1 2.4 %collective-permute-start.3 = (f32[256,128]{1,0:T(8,128)S(1)}, f32[256,128]{1,0:T(8,128)S(1)}, u32[]{:S(2)}, u32[]{:S(2)}) collective-permute-start(f32[256,128]{1,0:T(8,128)S(1)} %get-tuple-element.22.refs_2_), channel_id=1, source_target_pairs={{0,1},{1,2},{2,3},{3,0},{4,5},{5,6},{6,7},{7,4},{8,9},{9,10},{10,1... | collective-permute-start | bytes 393224 | tf_op jit(solution)/shard_map/ppermute | solution.py:324
  76.1 2.4 %collective-permute-done.2.refs_4_ = f32[256,128]{1,0:T(8,128)S(1)} collective-permute-done((f32[256,128]{1,0:T(8,128)S(1)}, f32[256,128]{1,0:T(8,128)S(1)}, u32[]{:S(2)}, u32[]{:S(2)}) %collective-permute-start.2) | collective-permute-done | bytes 131104 | tf_op jit(solution)/shard_map/ppermute | solution.py:324
  78.5 2.5 %collective-permute-done.3.refs_5_ = f32[256,128]{1,0:T(8,128)S(1)} collective-permute-done((f32[256,128]{1,0:T(8,128)S(1)}, f32[256,128]{1,0:T(8,128)S(1)}, u32[]{:S(2)}, u32[]{:S(2)}) %collective-permute-start.3) | collective-permute-done | bytes 131104 | tf_op jit(solution)/shard_map/ppermute | solution.py:324
  81.1 15.6 %all-to-all-done = f32[64,4,128]{2,1,0:T(4,128)S(1)} async-done(((f32[64,4,128]{2,1,0:T(4,128)}), f32[64,4,128]{2,1,0:T(4,128)S(1)}, u32[]{:S(2)}, u32[]{:S(2)}) %all-to-all-start) | async-done | bytes 131104 | tf_op jit(solution)/shard_map/all_to_all | solution.py:374
  97.9 14.5 %shard_map.89 = (f32[256,128]{1,0:T(8,128)}, f32[128,128]{1,0:T(8,128)}, f32[512,128]{1,0:T(8,128)}, f32[128,128]{1,0:T(8,128)}, f32[128,128]{1,0:T(8,128)}, /*index=5*/f32[128,128]{1,0:T(8,128)}, f32[128,128]{1,0:T(8,128)}) custom-call(s32[13]{0:T(128)} %pad_add_fusion.order_ref, f32[656,128]{1,0:T(8,128)} %copy-done.1, f32[256,128]{1,0:T(8,128)} %bitcast.36, ...), custom_call_target="tpu_custom_call" | custom-call | tf_op jit(solution)/shard_map/pallas_call | solution.py:291
  112.5 7.3 %all-to-all-start.1 = ((f32[64,4,128]{2,1,0:T(4,128)}), f32[64,4,128]{2,1,0:T(4,128)S(1)}, u32[]{:S(2)}, u32[]{:S(2)}) async-start(f32[64,4,128]{2,1,0:T(4,128)} %bitcast.38), calls=%async_computation.1 | async-start | bytes 262144 | tf_op jit(solution)/shard_map/all_to_all | solution.py:374
  119.8 4.1 %all-gather.1 = f32[1024,128]{1,0:T(8,128)S(1)} all-gather(f32[512,128]{1,0:T(8,128)S(1)} %copy-done.13), channel_id=3, replica_groups={{0,4},{8,12},{16,20},{24,28},{32,36},{40,44},{48,52},{56,60},{64,68},{7..., dimensions={0}, use_global_device_ids=true | all-gather | bytes 786432 | tf_op jit(solution)/shard_map/all_gather | solution.py:327
  124.0 3.6 %collective-permute-start.7 = (f32[128,128]{1,0:T(8,128)S(1)}, f32[128,128]{1,0:T(8,128)S(1)}, u32[]{:S(2)}, u32[]{:S(2)}) collective-permute-start(f32[128,128]{1,0:T(8,128)S(1)} %get-tuple-element.34), channel_id=1, source_target_pairs={{0,3},{1,0},{2,1},{3,2},{4,7},{5,4},{6,5},{7,6},{8,11},{9,8},{10,9... | collective-permute-start | bytes 196616 | tf_op jit(solution)/shard_map/ppermute | solution.py:324
  127.7 1.9 %collective-permute-start.8 = (f32[128,128]{1,0:T(8,128)S(1)}, f32[128,128]{1,0:T(8,128)S(1)}, u32[]{:S(2)}, u32[]{:S(2)}) collective-permute-start(f32[128,128]{1,0:T(8,128)S(1)} %get-tuple-element.35), channel_id=1, source_target_pairs={{0,2},{1,3},{2,0},{3,1},{4,6},{5,7},{6,4},{7,5},{8,10},{9,11},{10,... | collective-permute-start | bytes 196616 | tf_op jit(solution)/shard_map/ppermute | solution.py:324
  129.6 2.5 %collective-permute-start.9 = (f32[128,128]{1,0:T(8,128)S(1)}, f32[128,128]{1,0:T(8,128)S(1)}, u32[]{:S(2)}, u32[]{:S(2)}) collective-permute-start(f32[128,128]{1,0:T(8,128)S(1)} %get-tuple-element.36), channel_id=1, source_target_pairs={{0,1},{1,2},{2,3},{3,0},{4,5},{5,6},{6,7},{7,4},{8,9},{9,10},{10,1... | collective-permute-start | bytes 196616 | tf_op jit(solution)/shard_map/ppermute | solution.py:324
  132.1 2.4 %collective-permute-done.8 = f32[128,128]{1,0:T(8,128)S(1)} collective-permute-done((f32[128,128]{1,0:T(8,128)S(1)}, f32[128,128]{1,0:T(8,128)S(1)}, u32[]{:S(2)}, u32[]{:S(2)}) %collective-permute-start.8) | collective-permute-done | bytes 65568 | tf_op jit(solution)/shard_map/ppermute | solution.py:324
  134.5 1.8 %collective-permute-done.9 = f32[128,128]{1,0:T(8,128)S(1)} collective-permute-done((f32[128,128]{1,0:T(8,128)S(1)}, f32[128,128]{1,0:T(8,128)S(1)}, u32[]{:S(2)}, u32[]{:S(2)}) %collective-permute-start.9) | collective-permute-done | bytes 65568 | tf_op jit(solution)/shard_map/ppermute | solution.py:324
  138.0 3.1 %all-gather.2 = f32[256,128]{1,0:T(8,128)S(1)} all-gather(f32[128,128]{1,0:T(8,128)S(1)} %get-tuple-element.33), channel_id=4, replica_groups={{0,4},{8,12},{16,20},{24,28},{32,36},{40,44},{48,52},{56,60},{64,68},{7..., dimensions={0}, use_global_device_ids=true | all-gather | bytes 196608 | tf_op jit(solution)/shard_map/all_gather | solution.py:327
  (57 shorter events, 7.6 us)
Async XLA Ops:
  0.6 1.6 %copy-start.8 = (s32[128,2]{0,1:T(2,128)S(1)}, s32[128,2]{0,1:T(2,128)}, u32[]{:S(2)}) copy-start(s32[128,2]{0,1:T(2,128)} %param.13) | copy-start | bytes 3076
  0.7 14.3 %collective-permute-start = (f32[27,4,128]{2,1,0:T(4,128)}, f32[27,4,128]{2,1,0:T(4,128)S(1)}, u32[]{:S(2)}, u32[]{:S(2)}) collective-permute-start(f32[27,4,128]{2,1,0:T(4,128)} %param.8), channel_id=1, source_target_pairs={{0,0},{1,128},{2,256},{3,384},{4,4},{5,132},{6,260},{7,388},{8,8},... | collective-permute-start | bytes 165896 | tf_op jit(solution)/shard_map/ppermute | solution.py:337
  14.9 41.6 %copy-start.1 = (f32[656,128]{1,0:T(8,128)}, f32[656,128]{1,0:T(8,128)S(1)}, u32[]{:S(2)}) copy-start(f32[656,128]{1,0:T(8,128)S(1)} %all-gather.shared_ref.refs_0_) | copy-start | bytes 1007620
  43.7 54.2 %copy-start = (f32[27,64,128]{2,1,0:T(8,128)}, f32[27,64,128]{2,1,0:T(8,128)S(1)}, u32[]{:S(2)}) copy-start(f32[27,64,128]{2,1,0:T(8,128)S(1)} %shard_map.87.refs_6_) | copy-start | bytes 2654212
  43.8 52.9 %collective-permute-start.4 = (f32[27,64,128]{2,1,0:T(8,128)S(1)}, f32[27,64,128]{2,1,0:T(8,128)S(1)}, u32[]{:S(2)}, u32[]{:S(2)}) collective-permute-start(f32[27,64,128]{2,1,0:T(8,128)S(1)} %shard_map.87.refs_6_), channel_id=1, source_target_pairs={{0,384},{4,388},{8,392},{12,396},{16,400},{20,404},{24,408},{28,41... | collective-permute-start | bytes 2654216 | tf_op jit(solution)/shard_map/ppermute | solution.py:321
  51.3 45.4 %collective-permute-start.5 = (f32[27,64,128]{2,1,0:T(8,128)S(1)}, f32[27,64,128]{2,1,0:T(8,128)S(1)}, u32[]{:S(2)}, u32[]{:S(2)}) collective-permute-start(f32[27,64,128]{2,1,0:T(8,128)S(1)} %shard_map.87.refs_6_), channel_id=1, source_target_pairs={{0,256},{4,260},{8,264},{12,268},{16,272},{20,276},{24,280},{28,28... | collective-permute-start | bytes 2654216 | tf_op jit(solution)/shard_map/ppermute | solution.py:321
  53.8 43.0 %collective-permute-start.6 = (f32[27,64,128]{2,1,0:T(8,128)S(1)}, f32[27,64,128]{2,1,0:T(8,128)}, u32[]{:S(2)}, u32[]{:S(2)}) collective-permute-start(f32[27,64,128]{2,1,0:T(8,128)S(1)} %shard_map.87.refs_6_), channel_id=1, source_target_pairs={{0,128},{4,132},{8,136},{12,140},{16,144},{20,148},{24,152},{28,15... | collective-permute-start | bytes 2654216 | tf_op jit(solution)/shard_map/ppermute | solution.py:321
  57.6 15.5 %copy-start.2 = (f32[256,128]{1,0:T(8,128)}, f32[256,128]{1,0:T(8,128)S(1)}, u32[]{:S(2)}) copy-start(f32[256,128]{1,0:T(8,128)S(1)} %get-tuple-element.22.refs_2_) | copy-start | bytes 393220
  57.6 39.1 %all-to-all-start = ((f32[64,4,128]{2,1,0:T(4,128)}), f32[64,4,128]{2,1,0:T(4,128)S(1)}, u32[]{:S(2)}, u32[]{:S(2)}) async-start(f32[64,4,128]{2,1,0:T(4,128)} %bitcast.2), calls=%async_computation | async-start | bytes 262144 | tf_op jit(solution)/shard_map/all_to_all | solution.py:374
  66.1 7.0 %collective-permute-start.1 = (f32[256,128]{1,0:T(8,128)S(1)}, f32[256,128]{1,0:T(8,128)S(1)}, u32[]{:S(2)}, u32[]{:S(2)}) collective-permute-start(f32[256,128]{1,0:T(8,128)S(1)} %get-tuple-element.22.refs_2_), channel_id=1, source_target_pairs={{0,3},{1,0},{2,1},{3,2},{4,7},{5,4},{6,5},{7,6},{8,11},{9,8},{10,9... | collective-permute-start | bytes 393224 | tf_op jit(solution)/shard_map/ppermute | solution.py:324
  71.0 7.5 %collective-permute-start.2 = (f32[256,128]{1,0:T(8,128)S(1)}, f32[256,128]{1,0:T(8,128)S(1)}, u32[]{:S(2)}, u32[]{:S(2)}) collective-permute-start(f32[256,128]{1,0:T(8,128)S(1)} %get-tuple-element.22.refs_2_), channel_id=1, source_target_pairs={{0,2},{1,3},{2,0},{3,1},{4,6},{5,7},{6,4},{7,5},{8,10},{9,11},{10,... | collective-permute-start | bytes 393224 | tf_op jit(solution)/shard_map/ppermute | solution.py:324
  73.1 23.6 %copy-start.14 = (f32[256,128]{1,0:T(8,128)}, f32[256,128]{1,0:T(8,128)S(1)}, u32[]{:S(2)}) copy-start(f32[256,128]{1,0:T(8,128)S(1)} %collective-permute-done.1.refs_3_) | copy-start | bytes 393220
  73.1 7.9 %collective-permute-start.3 = (f32[256,128]{1,0:T(8,128)S(1)}, f32[256,128]{1,0:T(8,128)S(1)}, u32[]{:S(2)}, u32[]{:S(2)}) collective-permute-start(f32[256,128]{1,0:T(8,128)S(1)} %get-tuple-element.22.refs_2_), channel_id=1, source_target_pairs={{0,1},{1,2},{2,3},{3,0},{4,5},{5,6},{6,7},{7,4},{8,9},{9,10},{10,1... | collective-permute-start | bytes 393224 | tf_op jit(solution)/shard_map/ppermute | solution.py:324
  78.5 18.2 %copy-start.15 = (f32[256,128]{1,0:T(8,128)}, f32[256,128]{1,0:T(8,128)S(1)}, u32[]{:S(2)}) copy-start(f32[256,128]{1,0:T(8,128)S(1)} %collective-permute-done.2.refs_4_) | copy-start | bytes 393220
  81.0 15.7 %copy-start.16 = (f32[256,128]{1,0:T(8,128)}, f32[256,128]{1,0:T(8,128)S(1)}, u32[]{:S(2)}) copy-start(f32[256,128]{1,0:T(8,128)S(1)} %collective-permute-done.3.refs_5_) | copy-start | bytes 393220
  112.4 7.4 %copy-start.13 = (f32[512,128]{1,0:T(8,128)S(1)}, f32[512,128]{1,0:T(8,128)}, u32[]{:S(2)}) copy-start(f32[512,128]{1,0:T(8,128)} %get-tuple-element.25) | copy-start | bytes 786436
  112.5 24.5 %all-to-all-start.1 = ((f32[64,4,128]{2,1,0:T(4,128)}), f32[64,4,128]{2,1,0:T(4,128)S(1)}, u32[]{:S(2)}, u32[]{:S(2)}) async-start(f32[64,4,128]{2,1,0:T(4,128)} %bitcast.38), calls=%async_computation.1 | async-start | bytes 262144 | tf_op jit(solution)/shard_map/all_to_all | solution.py:374
  119.8 4.2 %copy-start.17 = (f32[128,128]{1,0:T(8,128)S(1)}, f32[128,128]{1,0:T(8,128)}, u32[]{:S(2)}) copy-start(f32[128,128]{1,0:T(8,128)} %get-tuple-element.28) | copy-start | bytes 196612
  119.8 4.2 %copy-start.18 = (f32[128,128]{1,0:T(8,128)S(1)}, f32[128,128]{1,0:T(8,128)}, u32[]{:S(2)}) copy-start(f32[128,128]{1,0:T(8,128)} %get-tuple-element.27) | copy-start | bytes 196612
  119.8 4.2 %copy-start.19 = (f32[128,128]{1,0:T(8,128)S(1)}, f32[128,128]{1,0:T(8,128)}, u32[]{:S(2)}) copy-start(f32[128,128]{1,0:T(8,128)} %get-tuple-element.26) | copy-start | bytes 196612
  124.0 12.3 %copy-start.20 = (f32[128,128]{1,0:T(8,128)S(1)}, f32[128,128]{1,0:T(8,128)}, u32[]{:S(2)}) copy-start(f32[128,128]{1,0:T(8,128)} %get-tuple-element.24) | copy-start | bytes 196612
  124.0 8.1 %collective-permute-start.7 = (f32[128,128]{1,0:T(8,128)S(1)}, f32[128,128]{1,0:T(8,128)S(1)}, u32[]{:S(2)}, u32[]{:S(2)}) collective-permute-start(f32[128,128]{1,0:T(8,128)S(1)} %get-tuple-element.34), channel_id=1, source_target_pairs={{0,3},{1,0},{2,1},{3,2},{4,7},{5,4},{6,5},{7,6},{8,11},{9,8},{10,9... | collective-permute-start | bytes 196616 | tf_op jit(solution)/shard_map/ppermute | solution.py:324
  127.7 6.8 %collective-permute-start.8 = (f32[128,128]{1,0:T(8,128)S(1)}, f32[128,128]{1,0:T(8,128)S(1)}, u32[]{:S(2)}, u32[]{:S(2)}) collective-permute-start(f32[128,128]{1,0:T(8,128)S(1)} %get-tuple-element.35), channel_id=1, source_target_pairs={{0,2},{1,3},{2,0},{3,1},{4,6},{5,7},{6,4},{7,5},{8,10},{9,11},{10,... | collective-permute-start | bytes 196616 | tf_op jit(solution)/shard_map/ppermute | solution.py:324
  129.6 6.7 %collective-permute-start.9 = (f32[128,128]{1,0:T(8,128)S(1)}, f32[128,128]{1,0:T(8,128)S(1)}, u32[]{:S(2)}, u32[]{:S(2)}) collective-permute-start(f32[128,128]{1,0:T(8,128)S(1)} %get-tuple-element.36), channel_id=1, source_target_pairs={{0,1},{1,2},{2,3},{3,0},{4,5},{5,6},{6,7},{7,4},{8,9},{9,10},{10,1... | collective-permute-start | bytes 196616 | tf_op jit(solution)/shard_map/ppermute | solution.py:324
  (9 other events, 8.4 us)

commit v2 on v1

--- a/solution.py
+++ b/solution.py
@@ -9,7 +9,8 @@
 BF16 = jnp.bfloat16
 NY = 4
 CORES = 2
-CHUNKS = 3
+SPANS = ((0, 9), (9, 18), (18, 27))
+CHUNKS = len(SPANS)
 SMALL, LARGE = 16, 63
 
 
@@ -31,6 +32,18 @@
 
 def dot(a, b):
     return jnp.dot(a, b, preferred_element_type=F32)
+
+
+def chip_x():
+    return lax.axis_index("chan")
+
+
+def chip_y():
+    return lax.axis_index("space") // (lax.axis_size("space") // NY)
+
+
+def core_index():
+    return lax.axis_index("space") % CORES
 
 
 def as_onehot(mask):
@@ -100,7 +113,7 @@
     shared_ref[SENDS : SENDS + send_ref.shape[0], :] = send_ref[...].astype(F32)
 
 
-def outgoing_kernel(core_ref, shared_ref, outgoing_ref, cot_ref, sends_ref, picked_ref):
+def outgoing_kernel(shared_ref, outgoing_ref, cot_ref, sends_ref, picked_ref):
     rows, width = picked_ref.shape
     half = width // CORES
     slots = sends_ref.shape[0] // CORES
@@ -109,7 +122,7 @@
         base = device * SHARED
         cot_ref[device * rows : (device + 1) * rows, :] = shared_ref[base : base + rows, :]
         inner = shared_ref[base + FEATURES : base + FEATURES + rows, :]
-        parts = split3(pltpu.roll(inner, half * core_ref[0], axis=1))
+        parts = split3(pltpu.roll(inner, half * core_index(), axis=1))
         for slot in range(slots):
             line = shared_ref[base + SENDS + slot : base + SENDS + slot + 1, :]
             sends_ref[device * slots + slot : device * slots + slot + 1, :] = line
@@ -147,87 +160,94 @@
     return wide.reshape(wide.shape[0] * wide.shape[1], wide.shape[2])
 
 
-def core_kernel(order_ref, *refs):
+def core_kernel(*refs):
     shared_in, incoming_in = refs[:2]
-    cot_in = refs[2 : NY + 2]
-    piece_in = refs[NY + 2 : 2 * NY + 2]
-    refs = refs[2 * NY + 2 :]
-    halo_out, local_ref, other_ref, *part_outs = refs[: NY + 3]
+    cot_in = refs[2]
+    piece_in = refs[3 : NY + 3]
+    refs = refs[NY + 3 :]
+    halo_out, local_ref, *part_outs = refs[: NY + 2]
     shared_ref, incoming_ref, cot_ref, pieces_ref, turned_ref, table_ref, total_ref, halo_ref = refs[
-        NY + 3 : -4
+        NY + 2 : -4
     ]
     first_sems, cot_sems, piece_sems, out_sems = refs[-4:]
-    rows, width = part_outs[0].shape
-    both_rows = CORES * rows
-    table_rows = table_ref.shape[0]
-    offsets = pieces_ref.shape[1]
+    both_rows, width = part_outs[0].shape
+    rows = both_rows // CORES
+    table_rows = table_ref.shape[0] // CORES
     half = pieces_ref.shape[2]
-    step = offsets // CHUNKS
-    core = order_ref[NY]
+    x, y, core = chip_x(), chip_y(), core_index()
 
     def piece_copy(chunk, n):
-        span = pl.ds(chunk * step, step)
+        span = pl.ds(SPANS[chunk][0], SPANS[chunk][1] - SPANS[chunk][0])
         return pltpu.make_async_copy(piece_in[n].at[span], pieces_ref.at[n, span], piece_sems.at[chunk, n])
 
-    first = [
-        pltpu.make_async_copy(shared_in, shared_ref, first_sems.at[0]),
-        pltpu.make_async_copy(incoming_in, incoming_ref, first_sems.at[1]),
+    shared_copy = pltpu.make_async_copy(shared_in, shared_ref, first_sems.at[0])
+    incoming_copy = pltpu.make_async_copy(incoming_in, incoming_ref, first_sems.at[1])
+    cots = [
+        pltpu.make_async_copy(cot_in.at[(y + n) % NY], cot_ref.at[n], cot_sems.at[n]) for n in range(NY)
     ]
-    cots = [
-        pltpu.make_async_copy(cot_in[m], cot_ref.at[m], cot_sems.at[m])
-        for m in range(NY)
-    ]
-    for copy in first + cots:
+    for copy in [shared_copy, incoming_copy] + cots:
         copy.start()
     for chunk in range(CHUNKS):
         for n in range(NY):
             piece_copy(chunk, n).start()
-    for copy in first + cots:
-        copy.wait()
-    for n in range(NY):
-        high, low = split2(cot_ref[order_ref[NY + 1 + n]].T)
-        turned_ref[n * width : (n + 1) * width, :both_rows] = high
-        turned_ref[n * width : (n + 1) * width, both_rows:] = low
+
+    def pairs_at(chunk):
+        return [
+            jnp.concatenate(
+                [pairs_of(shared_ref, d, k, rows, table_rows) for k in range(*SPANS[chunk])], axis=0
+            )
+            for d in range(CORES)
+        ]
+
+    shared_copy.wait()
     local = [
         pltpu.roll(
             shared_ref[d * SHARED + FEATURES : d * SHARED + FEATURES + rows, :], half * core, axis=1
         )[:, :half]
         for d in range(CORES)
     ]
+    incoming_copy.wait()
     table = jnp.concatenate([jnp.concatenate(local, axis=1), incoming_ref[...]], axis=0)
     high, low = split2(table)
-    table_ref[:, :width] = high
-    table_ref[:, width:] = low
+    table_ref[...] = jnp.zeros_like(table_ref)
+    for d in range(CORES):
+        mine = slice(d * half, (d + 1) * half)
+        table_ref[d * table_rows : (d + 1) * table_rows, d * width : (d + 1) * width] = jnp.concatenate(
+            [high[:, mine], low[:, mine]], axis=1
+        )
+    for copy in cots:
+        copy.wait()
+    for n in range(NY):
+        high, low = split2(cot_ref[n].T)
+        turned_ref[n * width : (n + 1) * width, :both_rows] = high
+        turned_ref[n * width : (n + 1) * width, both_rows:] = low
 
     grads = [None] * CORES
     total = None
     for chunk in range(CHUNKS):
-        pairs = [
+        step = SPANS[chunk][1] - SPANS[chunk][0]
+        pairs = pairs_at(chunk)
+        both = dot(jnp.concatenate(pairs, axis=1), table_ref[...]).astype(BF16)
+        wide = [
             jnp.concatenate(
-                [pairs_of(shared_ref, d, chunk * step + k, rows, table_rows) for k in range(step)], axis=0
+                [both[k * rows : (k + 1) * rows, d * width : (d + 1) * width] for k in range(step)], axis=1
             )
             for d in range(CORES)
         ]
-        picked = []
-        for device in range(CORES):
-            both = dot(pairs[device], table_ref[...]).astype(BF16)
-            for start in (device * half, width + device * half):
-                picked.append(
-                    jnp.concatenate(
-                        [both[k * rows : (k + 1) * rows, start : start + half] for k in range(step)],
-                        axis=1,
-                    )
-                )
-        highs = jnp.concatenate([picked[0], picked[2]], axis=0)
-        lows = jnp.concatenate([picked[1], picked[3]], axis=0)
+        wide = jnp.concatenate(wide, axis=0)
         for n in range(NY):
             piece_copy(chunk, n).wait()
-        span = slice(chunk * step, (chunk + 1) * step)
+        span = slice(*SPANS[chunk])
         high, low = split2(kernel_rows([pieces_ref[n, span] for n in range(NY)]))
-        product = dot(highs, high) + dot(lows, high) + dot(highs, low)
+
+        def doubled(x):
+            x = x.reshape(step, half, x.shape[1])
+            return jnp.concatenate([x, x], axis=1).reshape(step * width, x.shape[2])
+
+        product = dot(wide, doubled(high)) + dot(wide, doubled(low))
         total = product if chunk == 0 else total + product
-        wide = dot(high, turned_ref[...])
-        product = wide[:, :both_rows] + wide[:, both_rows:] + dot(low, turned_ref[:, :both_rows])
+        turned = dot(high, turned_ref[...])
+        product = turned[:, :both_rows] + turned[:, both_rows:] + dot(low, turned_ref[:, :both_rows])
         product = product.reshape(step, half, both_rows)
         for device in range(CORES):
             side = jnp.concatenate(
@@ -242,29 +262,29 @@
     outs[0].start()
     local_ref[...] = table[:rows, :]
     for n in range(NY):
-        for device in range(CORES):
-            part = total[device * rows : (device + 1) * rows, n * width : (n + 1) * width]
-            total_ref[device, n] = part
+        total_ref[n] = total[:, n * width : (n + 1) * width]
     for s in range(NY):
         outs.append(
-            pltpu.make_async_copy(
-                total_ref.at[core, order_ref[2 * NY + 1 + s]], part_outs[s], out_sems.at[s]
-            )
+            pltpu.make_async_copy(total_ref.at[(x + s - y + NY) % NY], part_outs[s], out_sems.at[s])
         )
         outs[-1].start()
-        other_ref[s * rows : (s + 1) * rows, :] = total_ref[1 - core, order_ref[2 * NY + 1 + s]]
     for copy in outs:
         copy.wait()
 
 
-def finish_kernel(core_ref, local_ref, returned_ref, sends_ref, own_ref, other_ref, grads_ref, full_ref):
-    rows, width = own_ref.shape
+def finish_kernel(local_ref, returned_ref, sends_ref, *refs):
+    part_refs = refs[:NY]
+    own_conv_ref, own_grad_ref, other_ref, grads_ref, convs_ref, full_ref = refs[NY:]
+    rows, width = own_grad_ref.shape
     half = width // CORES
     slots = sends_ref.shape[0] // CORES
     chips = sends_ref.shape[1] // CORES
+    core = core_index()
+    conv = (part_refs[0][...] + part_refs[1][...]) + (part_refs[2][...] + part_refs[3][...])
     spread = from_inner(width)
-    spread = jnp.where(core_ref[0] == 0, spread[:half, :], spread[half:, :])
+    spread = jnp.where(core == 0, spread[:half, :], spread[half:, :])
     for device in range(CORES):
+        convs_ref[device] = conv[device * rows : (device + 1) * rows, :]
         total = local_ref[:, device * half : (device + 1) * half]
         for slot in range(slots):
             line = device * slots + slot
@@ -274,8 +294,10 @@
             onehot = onehot_rows(sends_ref[line : line + 1, :], rows)
             total = total + pick_left(onehot, grads_ref[:, :half])
         full_ref[device] = pick_right(total, spread)
-    own_ref[...] = full_ref[core_ref[0]]
-    other_ref[...] = full_ref[1 - core_ref[0]]
+    own_conv_ref[...] = convs_ref[core]
+    own_grad_ref[...] = full_ref[core]
+    other_ref[:rows, :] = convs_ref[1 - core]
+    other_ref[rows:, :] = full_ref[1 - core]
 
 
 VMEM = pl.BlockSpec(memory_space=pltpu.VMEM)
@@ -325,14 +347,6 @@
 
     def of_chip(x):
         return lax.all_gather(x, "space", axis=0, tiled=False, axis_index_groups=chip_groups)
-
-    y = lax.axis_index("space") // (nz * CORES)
-    core = lax.axis_index("space") % CORES
-    turn = jnp.arange(NY, dtype=jnp.int32)
-    x = lax.axis_index("chan")
-    order = [(y + turn) % NY, core[None], (y + turn - x) % NY, (x + turn - y) % NY]
-    order = jnp.concatenate(order).astype(jnp.int32)
-    core = core[None]
 
     swapped = lax.ppermute(
         weights,
@@ -362,12 +376,11 @@
     outgoing, cots, sends = whole(
         outgoing_kernel,
         [((halo_rows, width), F32), ((CORES * rows, width), F32), ((CORES * slots, peers), F32)],
-        (core, shared),
-        in_specs=[SMEM, VMEM],
+        (shared,),
         scratch=[pltpu.VMEM((peers, width), F32)],
         mebibytes=SMALL,
     )
-    cots = [cots] + [along_x(cots, s) for s in (1, 2, 3)]
+    cots = lax.all_gather(cots, "chan", axis=0, tiled=False)
 
     def exchange(x):
         x = x.reshape(peers // CORES, CORES * slots, width)
@@ -377,21 +390,20 @@
         return x.reshape(halo_rows, width)
 
     incoming = exchange(outgoing)
-    halo_grad, local_grad, other_parts, *parts = whole(
+    halo_grad, local_grad, *parts = whole(
         core_kernel,
-        [((halo_rows, width), F32), ((rows, width), F32), ((NY * rows, width), F32)]
-        + [((rows, width), F32)] * NY,
-        (order, shared, incoming, *cots, *pieces),
-        in_specs=[SMEM] + [HBM] * (2 * NY + 2),
-        out_specs=[HBM] + [VMEM] * 2 + [HBM] * NY,
+        [((halo_rows, width), F32), ((rows, width), F32)] + [((CORES * rows, width), F32)] * NY,
+        (shared, incoming, cots, *pieces),
+        in_specs=[HBM] * (NY + 3),
+        out_specs=[HBM, VMEM] + [HBM] * NY,
         scratch=[
             pltpu.VMEM(shared.shape, F32),
             pltpu.VMEM(incoming.shape, F32),
             pltpu.VMEM((NY, CORES * rows, width), F32),
             pltpu.VMEM((NY, *own.shape), F32),
             pltpu.VMEM((NY * width, 2 * CORES * rows), BF16),
-            pltpu.VMEM((table_rows, 2 * width), BF16),
-            pltpu.VMEM((CORES, NY, rows, width), F32),
+            pltpu.VMEM((CORES * table_rows, 2 * width), BF16),
+            pltpu.VMEM((NY, CORES * rows, width), F32),
             pltpu.VMEM((halo_rows, width), F32),
             pltpu.SemaphoreType.DMA((2,)),
             pltpu.SemaphoreType.DMA((NY,)),
@@ -401,19 +413,21 @@
         mebibytes=LARGE,
     )
     returned = exchange(halo_grad)
-    other_parts = lax.dynamic_index_in_dim(of_chip(other_parts), 1 - core[0], 0, False)
-    parts = [p + other_parts[s * rows : (s + 1) * rows] for s, p in enumerate(parts)]
-    conv_out = parts[0] + along_x(parts[3], 1) + along_x(parts[2], 2) + along_x(parts[1], 3)
-    own_grad, other_grad = whole(
+    parts = [parts[0]] + [along_x(parts[NY - s], s) for s in (1, 2, 3)]
+    own_conv, own_grad, other = whole(
         finish_kernel,
-        [((rows, width), F32)] * 2,
-        (core, local_grad, returned, sends),
-        in_specs=[SMEM] + [VMEM] * 3,
-        scratch=[pltpu.VMEM((peers, width), F32), pltpu.VMEM((CORES, rows, width), F32)],
+        [((rows, width), F32)] * 2 + [((CORES * rows, width), F32)],
+        (local_grad, returned, sends, *parts),
+        scratch=[
+            pltpu.VMEM((peers, width), F32),
+            pltpu.VMEM((CORES, rows, width), F32),
+            pltpu.VMEM((CORES, rows, width), F32),
+        ],
         mebibytes=SMALL,
     )
-    other_grad = lax.dynamic_index_in_dim(of_chip(other_grad), 1 - core[0], 0, False)
-    return (conv_out, own_grad + other_grad)
+    core = lax.axis_index("space") % CORES
+    other = lax.dynamic_index_in_dim(of_chip(other), 1 - core, 0, False)
+    return (own_conv + other[:rows], own_grad + other[rows:])
 
 
 def solution(mesh):

time: 143 us -> 138 us (0.965)
  starting transfers between devices: 47.5 us -> 39.4 us
  blocking collectives: 44.4 us -> 52 us
  Pallas kernels: 17.6 us -> 15.1 us
    all_gather x0 -> x1, blocking collectives: none -> 11.8 us  [on_device(): cots = lax.all_gather(cots, 'chan', axis=0, tiled=False)]
    ppermute x6 -> x3, starting transfers between devices: 17.3 us -> 9.29 us  [along_x(): lax.ppermute(x, 'chan', [(a, (a - step) % chan) for a in range(chan)])]
    all_gather x3 -> x2, blocking collectives: 15.8 us -> 11.5 us  [of_chip(): lax.all_gather(x, 'space', axis=0, tiled=False, axis_index_groups=chip_gr...]
    all_to_all x2, waiting for transfers between devices: 15.6 us -> 18.8 us  [exchange(): lax.all_to_all(x, 'space', split_axis=0, concat_axis=0, tiled=True, axis_...]
    pallas_call x5, Pallas kernels: 17.6 us -> 15.1 us  [whole(): pl.pallas_call(kernel, out_shape=tuple((jax.ShapeDtypeStruct(s, t) for s,...]
    ppermute x6 -> x3, waiting for transfers between devices: 9.1 us -> 6.65 us  [along_x(): lax.ppermute(x, 'chan', [(a, (a - step) % chan) for a in range(chan)])]
    unnamed x42 -> x26, local copies, waits for them, and re-layouts: 4.53 us -> 4.34 us
  transfers between devices with their start and end apart: 12 -> 9, of which waited for: 5 -> 3; matrix products, arithmetic and copies ran while one was open for 1% -> 0% of each run, Pallas kernels for 1% -> 1%
where the time goes in v2:
time: 138 us
  blocking collectives  52 us (38%)
  starting transfers between devices  39.4 us (29%)
  waiting for transfers between devices  25.4 us (18%)
  Pallas kernels  15.1 us (11%)
  local copies, waits for them, and re-layouts  4.34 us (3%)
    all_gather x1, blocking collectives, on_device(): lax.all_gather(swapped, 'space', axis=0, tiled=True, axis_index_groups=z_...  28.7 us
    all_to_all x2, waiting for transfers between devices, exchange(): lax.all_to_all(x, 'space', split_axis=0, concat_axis=0, tiled=True, axis_...  18.8 us
    all_to_all x2, starting transfers between devices, exchange(): lax.all_to_all(x, 'space', split_axis=0, concat_axis=0, tiled=True, axis_...  15.8 us
    pallas_call x5, Pallas kernels, whole(): pl.pallas_call(kernel, out_shape=tuple((jax.ShapeDtypeStruct(s, t) for s,...  15.1 us
    ppermute x3, starting transfers between devices, along_y(): lax.ppermute(x, 'space', [(place(y, z, c), place(y - step, z, c)) for y,...  12.8 us
    all_gather x1, blocking collectives, on_device(): cots = lax.all_gather(cots, 'chan', axis=0, tiled=False)  11.8 us
    all_gather x2, blocking collectives, of_chip(): lax.all_gather(x, 'space', axis=0, tiled=False, axis_index_groups=chip_gr...  11.5 us
    ppermute x3, starting transfers between devices, along_x(): lax.ppermute(x, 'chan', [(a, (a - step) % chan) for a in range(chan)])  9.29 us
  transfers between devices with their start and end apart: 9, of which 3 were waited for; matrix products, arithmetic and copies ran while one was open for 0% of the time, Pallas kernels for 1%

profile of v2, /device:TPU:1, one launch (start us, length us, event | category | flops | bytes accessed | tf_op | source)
XLA Modules:
  0.0 137.8 jit_solution(15565709528337861201)
XLA Ops:
  0.7 1.6 %collective-permute-start = (f32[27,4,128]{2,1,0:T(4,128)}, f32[27,4,128]{2,1,0:T(4,128)S(1)}, u32[]{:S(2)}, u32[]{:S(2)}) collective-permute-start(f32[27,4,128]{2,1,0:T(4,128)} %param.8), channel_id=1, source_target_pairs={{0,0},{1,128},{2,256},{3,384},{4,4},{5,132},{6,260},{7,388},{8,8},... | collective-permute-start | bytes 165896 | tf_op jit(solution)/shard_map/ppermute | solution.py:351
  2.3 0.8 copy-done.3
  3.1 0.8 copy-done.4
  3.9 0.7 copy-done.6
  5.4 1.0 shard_map.86
  6.4 8.6 %all-gather.shared_ref.refs_0_ = f32[656,128]{1,0:T(8,128)S(1)} all-gather(f32[328,128]{1,0:T(8,128)S(1)} %shard_map.86), channel_id=2, replica_groups={{0,4},{8,12},{16,20},{24,28},{32,36},{40,44},{48,52},{56,60},{64,68},{7..., dimensions={0}, use_global_device_ids=true | all-gather | bytes 503808 | tf_op jit(solution)/shard_map/all_gather | solution.py:349
  14.9 28.7 %all_gather.23.gathered_ref = f32[432,4,128]{2,1,0:T(4,128)S(1)} all-gather(f32[27,4,128]{2,1,0:T(4,128)S(1)} %collective-permute-done), channel_id=1, replica_groups={{0,8,16,24,32,40,48,56,64,72,80,88,96,104,112,120},{4,12,20,28,36,44,52..., dimensions={0}, use_global_device_ids=true | all-gather | bytes 940032 | tf_op jit(solution)/shard_map/all_gather | solution.py:372
  43.8 7.5 %collective-permute-start.1 = (f32[27,64,128]{2,1,0:T(8,128)S(1)}, f32[27,64,128]{2,1,0:T(8,128)S(1)}, u32[]{:S(2)}, u32[]{:S(2)}) collective-permute-start(f32[27,64,128]{2,1,0:T(8,128)S(1)} %shard_map.87.refs_3_), channel_id=1, source_target_pairs={{0,384},{4,388},{8,392},{12,396},{16,400},{20,404},{24,408},{28,41... | collective-permute-start | bytes 2654216 | tf_op jit(solution)/shard_map/ppermute | solution.py:343
  51.3 2.5 %collective-permute-start.2 = (f32[27,64,128]{2,1,0:T(8,128)S(1)}, f32[27,64,128]{2,1,0:T(8,128)S(1)}, u32[]{:S(2)}, u32[]{:S(2)}) collective-permute-start(f32[27,64,128]{2,1,0:T(8,128)S(1)} %shard_map.87.refs_3_), channel_id=1, source_target_pairs={{0,256},{4,260},{8,264},{12,268},{16,272},{20,276},{24,280},{28,28... | collective-permute-start | bytes 2654216 | tf_op jit(solution)/shard_map/ppermute | solution.py:343
  53.8 2.8 %collective-permute-start.3 = (f32[27,64,128]{2,1,0:T(8,128)S(1)}, f32[27,64,128]{2,1,0:T(8,128)}, u32[]{:S(2)}, u32[]{:S(2)}) collective-permute-start(f32[27,64,128]{2,1,0:T(8,128)S(1)} %shard_map.87.refs_3_), channel_id=1, source_target_pairs={{0,128},{4,132},{8,136},{12,140},{16,144},{20,148},{24,152},{28,15... | collective-permute-start | bytes 2654216 | tf_op jit(solution)/shard_map/ppermute | solution.py:343
  56.5 1.1 shard_map.88
  57.6 8.5 %all-to-all-start = ((f32[64,4,128]{2,1,0:T(4,128)}), f32[64,4,128]{2,1,0:T(4,128)S(1)}, u32[]{:S(2)}, u32[]{:S(2)}) async-start(f32[64,4,128]{2,1,0:T(4,128)} %bitcast.1), calls=%async_computation | async-start | bytes 262144 | tf_op jit(solution)/shard_map/all_to_all | solution.py:387
  66.1 11.8 %all-gather.1 = f32[1024,128]{1,0:T(8,128)} all-gather(f32[256,128]{1,0:T(8,128)S(1)} %get-tuple-element.22), channel_id=3, replica_groups=mesh['space'=128,'chan'=4] {'chan'}, dimensions={0}, use_global_device_ids=true | all-gather | bytes 655360 | tf_op jit(solution)/shard_map/all_gather | solution.py:383
  77.9 18.8 %all-to-all-done = f32[64,4,128]{2,1,0:T(4,128)S(1)} async-done(((f32[64,4,128]{2,1,0:T(4,128)}), f32[64,4,128]{2,1,0:T(4,128)S(1)}, u32[]{:S(2)}, u32[]{:S(2)}) %all-to-all-start) | async-done | bytes 131104 | tf_op jit(solution)/shard_map/all_to_all | solution.py:387
  96.7 0.9 copy-done.10
  97.9 12.0 %shard_map.89 = (f32[256,128]{1,0:T(8,128)}, f32[128,128]{1,0:T(8,128)}, f32[256,128]{1,0:T(8,128)}, f32[256,128]{1,0:T(8,128)}, f32[256,128]{1,0:T(8,128)}, /*index=5*/f32[256,128]{1,0:T(8,128)}) custom-call(f32[656,128]{1,0:T(8,128)} %copy-done.1, f32[256,128]{1,0:T(8,128)} %bitcast.19, f32[4,256,128]{2,1,0:T(8,128)} %bitcast.17, f32[27,64,128]{2,1,0:T(8,128)} %copy-done, ...), custom_call_target="tpu_custom_call" | custom-call | tf_op jit(solution)/shard_map/pallas_call | solution.py:313
  109.9 7.3 %all-to-all-start.1 = ((f32[64,4,128]{2,1,0:T(4,128)}), f32[64,4,128]{2,1,0:T(4,128)S(1)}, u32[]{:S(2)}, u32[]{:S(2)}) async-start(f32[64,4,128]{2,1,0:T(4,128)} %bitcast.20), calls=%async_computation.1 | async-start | bytes 262144 | tf_op jit(solution)/shard_map/all_to_all | solution.py:387
  117.3 4.9 %collective-permute-start.4 = (f32[256,128]{1,0:T(8,128)}, f32[256,128]{1,0:T(8,128)S(1)}, u32[]{:S(2)}, u32[]{:S(2)}) collective-permute-start(f32[256,128]{1,0:T(8,128)} %get-tuple-element.28), channel_id=1, source_target_pairs={{0,3},{1,0},{2,1},{3,2},{4,7},{5,4},{6,5},{7,6},{8,11},{9,8},{10,9... | collective-permute-start | bytes 393224 | tf_op jit(solution)/shard_map/ppermute | solution.py:346
  122.2 2.0 %collective-permute-start.5 = (f32[256,128]{1,0:T(8,128)}, f32[256,128]{1,0:T(8,128)S(1)}, u32[]{:S(2)}, u32[]{:S(2)}) collective-permute-start(f32[256,128]{1,0:T(8,128)} %get-tuple-element.29), channel_id=1, source_target_pairs={{0,2},{1,3},{2,0},{3,1},{4,6},{5,7},{6,4},{7,5},{8,10},{9,11},{10,... | collective-permute-start | bytes 393224 | tf_op jit(solution)/shard_map/ppermute | solution.py:346
  124.2 2.4 %collective-permute-start.6 = (f32[256,128]{1,0:T(8,128)}, f32[256,128]{1,0:T(8,128)S(1)}, u32[]{:S(2)}, u32[]{:S(2)}) collective-permute-start(f32[256,128]{1,0:T(8,128)} %get-tuple-element.30), channel_id=1, source_target_pairs={{0,1},{1,2},{2,3},{3,0},{4,5},{5,6},{6,7},{7,4},{8,9},{9,10},{10,1... | collective-permute-start | bytes 393224 | tf_op jit(solution)/shard_map/ppermute | solution.py:346
  126.6 3.3 %collective-permute-done.5.refs_2_ = f32[256,128]{1,0:T(8,128)S(1)} collective-permute-done((f32[256,128]{1,0:T(8,128)}, f32[256,128]{1,0:T(8,128)S(1)}, u32[]{:S(2)}, u32[]{:S(2)}) %collective-permute-start.5) | collective-permute-done | bytes 131104 | tf_op jit(solution)/shard_map/ppermute | solution.py:346
  129.9 3.4 %collective-permute-done.6.refs_3_ = f32[256,128]{1,0:T(8,128)S(1)} collective-permute-done((f32[256,128]{1,0:T(8,128)}, f32[256,128]{1,0:T(8,128)S(1)}, u32[]{:S(2)}, u32[]{:S(2)}) %collective-permute-start.6) | collective-permute-done | bytes 131104 | tf_op jit(solution)/shard_map/ppermute | solution.py:346
  133.3 0.9 shard_map.90
  134.2 2.9 %all-gather.2 = f32[512,128]{1,0:T(8,128)S(1)} all-gather(f32[256,128]{1,0:T(8,128)S(1)} %get-tuple-element.32), channel_id=4, replica_groups={{0,4},{8,12},{16,20},{24,28},{32,36},{40,44},{48,52},{56,60},{64,68},{7..., dimensions={0}, use_global_device_ids=true | all-gather | bytes 393216 | tf_op jit(solution)/shard_map/all_gather | solution.py:349
  (30 shorter events, 1.9 us)
Async XLA Ops:
  0.6 1.6 %copy-start.8 = (s32[128,2]{0,1:T(2,128)S(1)}, s32[128,2]{0,1:T(2,128)}, u32[]{:S(2)}) copy-start(s32[128,2]{0,1:T(2,128)} %param.13) | copy-start | bytes 3076
  0.6 1.6 %copy-start.9 = (s32[27]{0:T(128)S(1)}, s32[27]{0:T(128)}, u32[]{:S(2)}) copy-start(s32[27]{0:T(128)} %count_ref.1) | copy-start | bytes 328
  0.7 14.3 %collective-permute-start = (f32[27,4,128]{2,1,0:T(4,128)}, f32[27,4,128]{2,1,0:T(4,128)S(1)}, u32[]{:S(2)}, u32[]{:S(2)}) collective-permute-start(f32[27,4,128]{2,1,0:T(4,128)} %param.8), channel_id=1, source_target_pairs={{0,0},{1,128},{2,256},{3,384},{4,4},{5,132},{6,260},{7,388},{8,8},... | collective-permute-start | bytes 165896 | tf_op jit(solution)/shard_map/ppermute | solution.py:351
  2.3 0.8 copy-start.3
  3.1 0.8 copy-start.4
  3.9 0.7 copy-start.6
  4.7 0.7 copy-start.7
  14.9 41.6 %copy-start.1 = (f32[656,128]{1,0:T(8,128)}, f32[656,128]{1,0:T(8,128)S(1)}, u32[]{:S(2)}) copy-start(f32[656,128]{1,0:T(8,128)S(1)} %all-gather.shared_ref.refs_0_) | copy-start | bytes 1007620
  43.7 54.2 %copy-start = (f32[27,64,128]{2,1,0:T(8,128)}, f32[27,64,128]{2,1,0:T(8,128)S(1)}, u32[]{:S(2)}) copy-start(f32[27,64,128]{2,1,0:T(8,128)S(1)} %shard_map.87.refs_3_) | copy-start | bytes 2654212
  43.8 52.9 %collective-permute-start.1 = (f32[27,64,128]{2,1,0:T(8,128)S(1)}, f32[27,64,128]{2,1,0:T(8,128)S(1)}, u32[]{:S(2)}, u32[]{:S(2)}) collective-permute-start(f32[27,64,128]{2,1,0:T(8,128)S(1)} %shard_map.87.refs_3_), channel_id=1, source_target_pairs={{0,384},{4,388},{8,392},{12,396},{16,400},{20,404},{24,408},{28,41... | collective-permute-start | bytes 2654216 | tf_op jit(solution)/shard_map/ppermute | solution.py:343
  51.3 45.4 %collective-permute-start.2 = (f32[27,64,128]{2,1,0:T(8,128)S(1)}, f32[27,64,128]{2,1,0:T(8,128)S(1)}, u32[]{:S(2)}, u32[]{:S(2)}) collective-permute-start(f32[27,64,128]{2,1,0:T(8,128)S(1)} %shard_map.87.refs_3_), channel_id=1, source_target_pairs={{0,256},{4,260},{8,264},{12,268},{16,272},{20,276},{24,280},{28,28... | collective-permute-start | bytes 2654216 | tf_op jit(solution)/shard_map/ppermute | solution.py:343
  53.8 43.0 %collective-permute-start.3 = (f32[27,64,128]{2,1,0:T(8,128)S(1)}, f32[27,64,128]{2,1,0:T(8,128)}, u32[]{:S(2)}, u32[]{:S(2)}) collective-permute-start(f32[27,64,128]{2,1,0:T(8,128)S(1)} %shard_map.87.refs_3_), channel_id=1, source_target_pairs={{0,128},{4,132},{8,136},{12,140},{16,144},{20,148},{24,152},{28,15... | collective-permute-start | bytes 2654216 | tf_op jit(solution)/shard_map/ppermute | solution.py:343
  57.6 39.1 %all-to-all-start = ((f32[64,4,128]{2,1,0:T(4,128)}), f32[64,4,128]{2,1,0:T(4,128)S(1)}, u32[]{:S(2)}, u32[]{:S(2)}) async-start(f32[64,4,128]{2,1,0:T(4,128)} %bitcast.1), calls=%async_computation | async-start | bytes 262144 | tf_op jit(solution)/shard_map/all_to_all | solution.py:387
  96.7 1.0 copy-start.12
  96.7 1.0 copy-start.10
  96.7 1.2 copy-start.11
  109.9 23.4 %copy-start.2 = (f32[256,128]{1,0:T(8,128)S(1)}, f32[256,128]{1,0:T(8,128)}, u32[]{:S(2)}) copy-start(f32[256,128]{1,0:T(8,128)} %get-tuple-element.27.refs_0_) | copy-start | bytes 393220
  109.9 23.4 %copy-start.5 = (f32[128,128]{1,0:T(8,128)S(1)}, f32[128,128]{1,0:T(8,128)}, u32[]{:S(2)}) copy-start(f32[128,128]{1,0:T(8,128)} %get-tuple-element.24.local_ref) | copy-start | bytes 196612
  109.9 23.3 %all-to-all-start.1 = ((f32[64,4,128]{2,1,0:T(4,128)}), f32[64,4,128]{2,1,0:T(4,128)S(1)}, u32[]{:S(2)}, u32[]{:S(2)}) async-start(f32[64,4,128]{2,1,0:T(4,128)} %bitcast.20), calls=%async_computation.1 | async-start | bytes 262144 | tf_op jit(solution)/shard_map/all_to_all | solution.py:387
  117.3 9.3 %collective-permute-start.4 = (f32[256,128]{1,0:T(8,128)}, f32[256,128]{1,0:T(8,128)S(1)}, u32[]{:S(2)}, u32[]{:S(2)}) collective-permute-start(f32[256,128]{1,0:T(8,128)} %get-tuple-element.28), channel_id=1, source_target_pairs={{0,3},{1,0},{2,1},{3,2},{4,7},{5,4},{6,5},{7,6},{8,11},{9,8},{10,9... | collective-permute-start | bytes 393224 | tf_op jit(solution)/shard_map/ppermute | solution.py:346
  122.2 7.7 %collective-permute-start.5 = (f32[256,128]{1,0:T(8,128)}, f32[256,128]{1,0:T(8,128)S(1)}, u32[]{:S(2)}, u32[]{:S(2)}) collective-permute-start(f32[256,128]{1,0:T(8,128)} %get-tuple-element.29), channel_id=1, source_target_pairs={{0,2},{1,3},{2,0},{3,1},{4,6},{5,7},{6,4},{7,5},{8,10},{9,11},{10,... | collective-permute-start | bytes 393224 | tf_op jit(solution)/shard_map/ppermute | solution.py:346
  124.2 9.1 %collective-permute-start.6 = (f32[256,128]{1,0:T(8,128)}, f32[256,128]{1,0:T(8,128)S(1)}, u32[]{:S(2)}, u32[]{:S(2)}) collective-permute-start(f32[256,128]{1,0:T(8,128)} %get-tuple-element.30), channel_id=1, source_target_pairs={{0,1},{1,2},{2,3},{3,0},{4,5},{5,6},{6,7},{7,4},{8,9},{9,10},{10,1... | collective-permute-start | bytes 393224 | tf_op jit(solution)/shard_map/ppermute | solution.py:346

commit v3 on v2

--- a/solution.py
+++ b/solution.py
@@ -9,7 +9,7 @@
 BF16 = jnp.bfloat16
 NY = 4
 CORES = 2
-SPANS = ((0, 9), (9, 18), (18, 27))
+SPANS = ((0, 6), (6, 27))
 CHUNKS = len(SPANS)
 SMALL, LARGE = 16, 63
 
@@ -187,10 +187,6 @@
     ]
     for copy in [shared_copy, incoming_copy] + cots:
         copy.start()
-    for chunk in range(CHUNKS):
-        for n in range(NY):
-            piece_copy(chunk, n).start()
-
     def pairs_at(chunk):
         return [
             jnp.concatenate(
@@ -200,6 +196,9 @@
         ]
 
     shared_copy.wait()
+    for chunk in range(CHUNKS):
+        for n in range(NY):
+            piece_copy(chunk, n).start()
     local = [
         pltpu.roll(
             shared_ref[d * SHARED + FEATURES : d * SHARED + FEATURES + rows, :], half * core, axis=1
@@ -244,8 +243,18 @@
             x = x.reshape(step, half, x.shape[1])
             return jnp.concatenate([x, x], axis=1).reshape(step * width, x.shape[2])
 
-        product = dot(wide, doubled(high)) + dot(wide, doubled(low))
+        highs = jnp.concatenate([wide[:, k * width : k * width + half] for k in range(step)], axis=1)
+        product = dot(wide, doubled(high)) + dot(highs, low)
         total = product if chunk == 0 else total + product
+        if chunk == CHUNKS - 1:
+            outs = []
+            for n in range(NY):
+                total_ref[n] = total[:, n * width : (n + 1) * width]
+            for s in range(NY):
+                outs.append(
+                    pltpu.make_async_copy(total_ref.at[(x + s - y + NY) % NY], part_outs[s], out_sems.at[s])
+                )
+                outs[-1].start()
         turned = dot(high, turned_ref[...])
         product = turned[:, :both_rows] + turned[:, both_rows:] + dot(low, turned_ref[:, :both_rows])
         product = product.reshape(step, half, both_rows)
@@ -258,16 +267,9 @@
             grads[device] = both if chunk == 0 else grads[device] + both
     table = jnp.concatenate(grads, axis=0).T
     halo_ref[...] = table[rows:, :]
-    outs = [pltpu.make_async_copy(halo_ref, halo_out, out_sems.at[NY])]
-    outs[0].start()
+    outs.append(pltpu.make_async_copy(halo_ref, halo_out, out_sems.at[NY]))
+    outs[-1].start()
     local_ref[...] = table[:rows, :]
-    for n in range(NY):
-        total_ref[n] = total[:, n * width : (n + 1) * width]
-    for s in range(NY):
-        outs.append(
-            pltpu.make_async_copy(total_ref.at[(x + s - y + NY) % NY], part_outs[s], out_sems.at[s])
-        )
-        outs[-1].start()
     for copy in outs:
         copy.wait()
 
@@ -413,7 +415,7 @@
         mebibytes=LARGE,
     )
     returned = exchange(halo_grad)
-    parts = [parts[0]] + [along_x(parts[NY - s], s) for s in (1, 2, 3)]
+    parts = [parts[0]] + [along_x(parts[NY - s], s) for s in (2, 1, 3)]
     own_conv, own_grad, other = whole(
         finish_kernel,
         [((rows, width), F32)] * 2 + [((CORES * rows, width), F32)],

time: 138 us -> 136 us (0.986)
  Pallas kernels: 15.1 us -> 12.8 us
    pallas_call x5, Pallas kernels: 15.1 us -> 12.8 us  [whole(): pl.pallas_call(kernel, out_shape=tuple((jax.ShapeDtypeStruct(s, t) for s,...]
  transfers between devices with their start and end apart: 9 -> 9, of which waited for: 3 -> 3; matrix products, arithmetic and copies ran while one was open for 0% -> 0% of each run, Pallas kernels for 1% -> 2%
where the time goes in v3:
time: 136 us; the launch traced here: 135 us
  blocking collectives  52.9 us (39%)
  starting transfers between devices  39.6 us (29%)
  waiting for transfers between devices  24.3 us (18%)
  Pallas kernels  12.8 us (9%)
  local copies, waits for them, and re-layouts  4.34 us (3%)
    all_gather x1, blocking collectives, on_device(): lax.all_gather(swapped, 'space', axis=0, tiled=True, axis_index_groups=z_...  28.7 us
    all_to_all x2, waiting for transfers between devices, exchange(): lax.all_to_all(x, 'space', split_axis=0, concat_axis=0, tiled=True, axis_...  18.8 us
    all_to_all x2, starting transfers between devices, exchange(): lax.all_to_all(x, 'space', split_axis=0, concat_axis=0, tiled=True, axis_...  15.8 us
    pallas_call x5, Pallas kernels, whole(): pl.pallas_call(kernel, out_shape=tuple((jax.ShapeDtypeStruct(s, t) for s,...  12.8 us
    ppermute x3, starting transfers between devices, along_y(): lax.ppermute(x, 'space', [(place(y, z, c), place(y - step, z, c)) for y,...  12.8 us
    all_gather x2, blocking collectives, of_chip(): lax.all_gather(x, 'space', axis=0, tiled=False, axis_index_groups=chip_gr...  12.4 us
    all_gather x1, blocking collectives, on_device(): cots = lax.all_gather(cots, 'chan', axis=0, tiled=False)  11.8 us
    ppermute x3, starting transfers between devices, along_x(): lax.ppermute(x, 'chan', [(a, (a - step) % chan) for a in range(chan)])  9.43 us
  transfers between devices with their start and end apart: 9, of which 3 were waited for; matrix products, arithmetic and copies ran while one was open for 0% of the time, Pallas kernels for 2%

profile of v3, /device:TPU:1, one launch (start us, length us, event | category | flops | bytes accessed | tf_op | source)
XLA Modules:
  0.0 135.4 jit_solution(10818527368594911075)
XLA Ops:
  0.7 1.6 %collective-permute-start = (f32[27,4,128]{2,1,0:T(4,128)}, f32[27,4,128]{2,1,0:T(4,128)S(1)}, u32[]{:S(2)}, u32[]{:S(2)}) collective-permute-start(f32[27,4,128]{2,1,0:T(4,128)} %param.8), channel_id=1, source_target_pairs={{0,0},{1,128},{2,256},{3,384},{4,4},{5,132},{6,260},{7,388},{8,8},... | collective-permute-start | bytes 165896 | tf_op jit(solution)/shard_map/ppermute | solution.py:353
  2.3 0.8 copy-done.3
  3.1 0.8 copy-done.4
  3.9 0.7 copy-done.6
  5.4 1.0 shard_map.86
  6.4 8.6 %all-gather.shared_ref.refs_0_ = f32[656,128]{1,0:T(8,128)S(1)} all-gather(f32[328,128]{1,0:T(8,128)S(1)} %shard_map.86), channel_id=2, replica_groups={{0,4},{8,12},{16,20},{24,28},{32,36},{40,44},{48,52},{56,60},{64,68},{7..., dimensions={0}, use_global_device_ids=true | all-gather | bytes 503808 | tf_op jit(solution)/shard_map/all_gather | solution.py:351
  14.9 28.7 %all_gather.23.gathered_ref = f32[432,4,128]{2,1,0:T(4,128)S(1)} all-gather(f32[27,4,128]{2,1,0:T(4,128)S(1)} %collective-permute-done), channel_id=1, replica_groups={{0,8,16,24,32,40,48,56,64,72,80,88,96,104,112,120},{4,12,20,28,36,44,52..., dimensions={0}, use_global_device_ids=true | all-gather | bytes 940032 | tf_op jit(solution)/shard_map/all_gather | solution.py:374
  43.8 7.5 %collective-permute-start.1 = (f32[27,64,128]{2,1,0:T(8,128)S(1)}, f32[27,64,128]{2,1,0:T(8,128)S(1)}, u32[]{:S(2)}, u32[]{:S(2)}) collective-permute-start(f32[27,64,128]{2,1,0:T(8,128)S(1)} %shard_map.87.refs_3_), channel_id=1, source_target_pairs={{0,384},{4,388},{8,392},{12,396},{16,400},{20,404},{24,408},{28,41... | collective-permute-start | bytes 2654216 | tf_op jit(solution)/shard_map/ppermute | solution.py:345
  51.3 2.5 %collective-permute-start.2 = (f32[27,64,128]{2,1,0:T(8,128)S(1)}, f32[27,64,128]{2,1,0:T(8,128)S(1)}, u32[]{:S(2)}, u32[]{:S(2)}) collective-permute-start(f32[27,64,128]{2,1,0:T(8,128)S(1)} %shard_map.87.refs_3_), channel_id=1, source_target_pairs={{0,256},{4,260},{8,264},{12,268},{16,272},{20,276},{24,280},{28,28... | collective-permute-start | bytes 2654216 | tf_op jit(solution)/shard_map/ppermute | solution.py:345
  53.8 2.8 %collective-permute-start.3 = (f32[27,64,128]{2,1,0:T(8,128)S(1)}, f32[27,64,128]{2,1,0:T(8,128)}, u32[]{:S(2)}, u32[]{:S(2)}) collective-permute-start(f32[27,64,128]{2,1,0:T(8,128)S(1)} %shard_map.87.refs_3_), channel_id=1, source_target_pairs={{0,128},{4,132},{8,136},{12,140},{16,144},{20,148},{24,152},{28,15... | collective-permute-start | bytes 2654216 | tf_op jit(solution)/shard_map/ppermute | solution.py:345
  56.5 1.1 shard_map.88
  57.6 8.5 %all-to-all-start = ((f32[64,4,128]{2,1,0:T(4,128)}), f32[64,4,128]{2,1,0:T(4,128)S(1)}, u32[]{:S(2)}, u32[]{:S(2)}) async-start(f32[64,4,128]{2,1,0:T(4,128)} %bitcast.1), calls=%async_computation | async-start | bytes 262144 | tf_op jit(solution)/shard_map/all_to_all | solution.py:389
  66.1 11.8 %all-gather.1 = f32[1024,128]{1,0:T(8,128)} all-gather(f32[256,128]{1,0:T(8,128)S(1)} %get-tuple-element.22), channel_id=3, replica_groups=mesh['space'=128,'chan'=4] {'chan'}, dimensions={0}, use_global_device_ids=true | all-gather | bytes 655360 | tf_op jit(solution)/shard_map/all_gather | solution.py:385
  77.9 18.8 %all-to-all-done = f32[64,4,128]{2,1,0:T(4,128)S(1)} async-done(((f32[64,4,128]{2,1,0:T(4,128)}), f32[64,4,128]{2,1,0:T(4,128)S(1)}, u32[]{:S(2)}, u32[]{:S(2)}) %all-to-all-start) | async-done | bytes 131104 | tf_op jit(solution)/shard_map/all_to_all | solution.py:389
  96.7 0.9 copy-done.10
  97.9 9.7 %shard_map.89 = (f32[256,128]{1,0:T(8,128)}, f32[128,128]{1,0:T(8,128)}, f32[256,128]{1,0:T(8,128)}, f32[256,128]{1,0:T(8,128)}, f32[256,128]{1,0:T(8,128)}, /*index=5*/f32[256,128]{1,0:T(8,128)}) custom-call(f32[656,128]{1,0:T(8,128)} %copy-done.1, f32[256,128]{1,0:T(8,128)} %bitcast.19, f32[4,256,128]{2,1,0:T(8,128)} %bitcast.17, f32[27,64,128]{2,1,0:T(8,128)} %copy-done, ...), custom_call_target="tpu_custom_call" | custom-call | tf_op jit(solution)/shard_map/pallas_call | solution.py:315
  107.7 7.3 %all-to-all-start.1 = ((f32[64,4,128]{2,1,0:T(4,128)}), f32[64,4,128]{2,1,0:T(4,128)S(1)}, u32[]{:S(2)}, u32[]{:S(2)}) async-start(f32[64,4,128]{2,1,0:T(4,128)} %bitcast.20), calls=%async_computation.1 | async-start | bytes 262144 | tf_op jit(solution)/shard_map/all_to_all | solution.py:389
  115.0 3.6 %collective-permute-start.4 = (f32[256,128]{1,0:T(8,128)}, f32[256,128]{1,0:T(8,128)S(1)}, u32[]{:S(2)}, u32[]{:S(2)}) collective-permute-start(f32[256,128]{1,0:T(8,128)} %get-tuple-element.28), channel_id=1, source_target_pairs={{0,2},{1,3},{2,0},{3,1},{4,6},{5,7},{6,4},{7,5},{8,10},{9,11},{10,... | collective-permute-start | bytes 393224 | tf_op jit(solution)/shard_map/ppermute | solution.py:348
  118.6 3.9 %collective-permute-start.5 = (f32[256,128]{1,0:T(8,128)}, f32[256,128]{1,0:T(8,128)S(1)}, u32[]{:S(2)}, u32[]{:S(2)}) collective-permute-start(f32[256,128]{1,0:T(8,128)} %get-tuple-element.29), channel_id=1, source_target_pairs={{0,3},{1,0},{2,1},{3,2},{4,7},{5,4},{6,5},{7,6},{8,11},{9,8},{10,9... | collective-permute-start | bytes 393224 | tf_op jit(solution)/shard_map/ppermute | solution.py:348
  122.6 1.9 %collective-permute-start.6 = (f32[256,128]{1,0:T(8,128)}, f32[256,128]{1,0:T(8,128)S(1)}, u32[]{:S(2)}, u32[]{:S(2)}) collective-permute-start(f32[256,128]{1,0:T(8,128)} %get-tuple-element.30), channel_id=1, source_target_pairs={{0,1},{1,2},{2,3},{3,0},{4,5},{5,6},{6,7},{7,4},{8,9},{9,10},{10,1... | collective-permute-start | bytes 393224 | tf_op jit(solution)/shard_map/ppermute | solution.py:348
  124.5 2.1 %collective-permute-done.5.refs_2_ = f32[256,128]{1,0:T(8,128)S(1)} collective-permute-done((f32[256,128]{1,0:T(8,128)}, f32[256,128]{1,0:T(8,128)S(1)}, u32[]{:S(2)}, u32[]{:S(2)}) %collective-permute-start.5) | collective-permute-done | bytes 131104 | tf_op jit(solution)/shard_map/ppermute | solution.py:348
  126.6 3.4 %collective-permute-done.6.refs_3_ = f32[256,128]{1,0:T(8,128)S(1)} collective-permute-done((f32[256,128]{1,0:T(8,128)}, f32[256,128]{1,0:T(8,128)S(1)}, u32[]{:S(2)}, u32[]{:S(2)}) %collective-permute-start.6) | collective-permute-done | bytes 131104 | tf_op jit(solution)/shard_map/ppermute | solution.py:348
  130.0 0.9 shard_map.90
  130.9 3.8 %all-gather.2 = f32[512,128]{1,0:T(8,128)S(1)} all-gather(f32[256,128]{1,0:T(8,128)S(1)} %get-tuple-element.32), channel_id=4, replica_groups={{0,4},{8,12},{16,20},{24,28},{32,36},{40,44},{48,52},{56,60},{64,68},{7..., dimensions={0}, use_global_device_ids=true | all-gather | bytes 393216 | tf_op jit(solution)/shard_map/all_gather | solution.py:351
  (30 shorter events, 1.9 us)
Async XLA Ops:
  0.6 1.6 %copy-start.8 = (s32[128,2]{0,1:T(2,128)S(1)}, s32[128,2]{0,1:T(2,128)}, u32[]{:S(2)}) copy-start(s32[128,2]{0,1:T(2,128)} %param.13) | copy-start | bytes 3076
  0.6 1.6 %copy-start.9 = (s32[27]{0:T(128)S(1)}, s32[27]{0:T(128)}, u32[]{:S(2)}) copy-start(s32[27]{0:T(128)} %count_ref.1) | copy-start | bytes 328
  0.7 14.3 %collective-permute-start = (f32[27,4,128]{2,1,0:T(4,128)}, f32[27,4,128]{2,1,0:T(4,128)S(1)}, u32[]{:S(2)}, u32[]{:S(2)}) collective-permute-start(f32[27,4,128]{2,1,0:T(4,128)} %param.8), channel_id=1, source_target_pairs={{0,0},{1,128},{2,256},{3,384},{4,4},{5,132},{6,260},{7,388},{8,8},... | collective-permute-start | bytes 165896 | tf_op jit(solution)/shard_map/ppermute | solution.py:353
  2.3 0.8 copy-start.3
  3.1 0.8 copy-start.4
  3.9 0.7 copy-start.6
  4.7 0.7 copy-start.7
  14.9 41.6 %copy-start.1 = (f32[656,128]{1,0:T(8,128)}, f32[656,128]{1,0:T(8,128)S(1)}, u32[]{:S(2)}) copy-start(f32[656,128]{1,0:T(8,128)S(1)} %all-gather.shared_ref.refs_0_) | copy-start | bytes 1007620
  43.7 54.2 %copy-start = (f32[27,64,128]{2,1,0:T(8,128)}, f32[27,64,128]{2,1,0:T(8,128)S(1)}, u32[]{:S(2)}) copy-start(f32[27,64,128]{2,1,0:T(8,128)S(1)} %shard_map.87.refs_3_) | copy-start | bytes 2654212
  43.8 52.9 %collective-permute-start.1 = (f32[27,64,128]{2,1,0:T(8,128)S(1)}, f32[27,64,128]{2,1,0:T(8,128)S(1)}, u32[]{:S(2)}, u32[]{:S(2)}) collective-permute-start(f32[27,64,128]{2,1,0:T(8,128)S(1)} %shard_map.87.refs_3_), channel_id=1, source_target_pairs={{0,384},{4,388},{8,392},{12,396},{16,400},{20,404},{24,408},{28,41... | collective-permute-start | bytes 2654216 | tf_op jit(solution)/shard_map/ppermute | solution.py:345
  51.3 45.4 %collective-permute-start.2 = (f32[27,64,128]{2,1,0:T(8,128)S(1)}, f32[27,64,128]{2,1,0:T(8,128)S(1)}, u32[]{:S(2)}, u32[]{:S(2)}) collective-permute-start(f32[27,64,128]{2,1,0:T(8,128)S(1)} %shard_map.87.refs_3_), channel_id=1, source_target_pairs={{0,256},{4,260},{8,264},{12,268},{16,272},{20,276},{24,280},{28,28... | collective-permute-start | bytes 2654216 | tf_op jit(solution)/shard_map/ppermute | solution.py:345
  53.8 43.0 %collective-permute-start.3 = (f32[27,64,128]{2,1,0:T(8,128)S(1)}, f32[27,64,128]{2,1,0:T(8,128)}, u32[]{:S(2)}, u32[]{:S(2)}) collective-permute-start(f32[27,64,128]{2,1,0:T(8,128)S(1)} %shard_map.87.refs_3_), channel_id=1, source_target_pairs={{0,128},{4,132},{8,136},{12,140},{16,144},{20,148},{24,152},{28,15... | collective-permute-start | bytes 2654216 | tf_op jit(solution)/shard_map/ppermute | solution.py:345
  57.6 39.1 %all-to-all-start = ((f32[64,4,128]{2,1,0:T(4,128)}), f32[64,4,128]{2,1,0:T(4,128)S(1)}, u32[]{:S(2)}, u32[]{:S(2)}) async-start(f32[64,4,128]{2,1,0:T(4,128)} %bitcast.1), calls=%async_computation | async-start | bytes 262144 | tf_op jit(solution)/shard_map/all_to_all | solution.py:389
  96.7 1.0 copy-start.12
  96.7 1.0 copy-start.10
  96.7 1.2 copy-start.11
  107.7 22.3 %copy-start.2 = (f32[256,128]{1,0:T(8,128)S(1)}, f32[256,128]{1,0:T(8,128)}, u32[]{:S(2)}) copy-start(f32[256,128]{1,0:T(8,128)} %get-tuple-element.27.refs_0_) | copy-start | bytes 393220
  107.7 22.3 %copy-start.5 = (f32[128,128]{1,0:T(8,128)S(1)}, f32[128,128]{1,0:T(8,128)}, u32[]{:S(2)}) copy-start(f32[128,128]{1,0:T(8,128)} %get-tuple-element.24.local_ref) | copy-start | bytes 196612
  107.7 22.3 %all-to-all-start.1 = ((f32[64,4,128]{2,1,0:T(4,128)}), f32[64,4,128]{2,1,0:T(4,128)S(1)}, u32[]{:S(2)}, u32[]{:S(2)}) async-start(f32[64,4,128]{2,1,0:T(4,128)} %bitcast.20), calls=%async_computation.1 | async-start | bytes 262144 | tf_op jit(solution)/shard_map/all_to_all | solution.py:389
  115.0 9.5 %collective-permute-start.4 = (f32[256,128]{1,0:T(8,128)}, f32[256,128]{1,0:T(8,128)S(1)}, u32[]{:S(2)}, u32[]{:S(2)}) collective-permute-start(f32[256,128]{1,0:T(8,128)} %get-tuple-element.28), channel_id=1, source_target_pairs={{0,2},{1,3},{2,0},{3,1},{4,6},{5,7},{6,4},{7,5},{8,10},{9,11},{10,... | collective-permute-start | bytes 393224 | tf_op jit(solution)/shard_map/ppermute | solution.py:348
  118.6 8.0 %collective-permute-start.5 = (f32[256,128]{1,0:T(8,128)}, f32[256,128]{1,0:T(8,128)S(1)}, u32[]{:S(2)}, u32[]{:S(2)}) collective-permute-start(f32[256,128]{1,0:T(8,128)} %get-tuple-element.29), channel_id=1, source_target_pairs={{0,3},{1,0},{2,1},{3,2},{4,7},{5,4},{6,5},{7,6},{8,11},{9,8},{10,9... | collective-permute-start | bytes 393224 | tf_op jit(solution)/shard_map/ppermute | solution.py:348
  122.6 7.4 %collective-permute-start.6 = (f32[256,128]{1,0:T(8,128)}, f32[256,128]{1,0:T(8,128)S(1)}, u32[]{:S(2)}, u32[]{:S(2)}) collective-permute-start(f32[256,128]{1,0:T(8,128)} %get-tuple-element.30), channel_id=1, source_target_pairs={{0,1},{1,2},{2,3},{3,0},{4,5},{5,6},{6,7},{7,4},{8,9},{9,10},{10,1... | collective-permute-start | bytes 393224 | tf_op jit(solution)/shard_map/ppermute | solution.py:348

commit v4 on v3

--- a/solution.py
+++ b/solution.py
@@ -367,7 +367,7 @@
             pltpu.VMEM(rule_dst.shape, jnp.int32),
             pltpu.SemaphoreType.DMA((5,)),
         ],
-        mebibytes=SMALL,
+        mebibytes=LARGE,
     )
     shared = of_chip(shared).reshape(CORES * SHARED, width)
     swapped, shared = lax.optimization_barrier((swapped, shared))

time: 136 us -> 135 us (level)
  local copies, waits for them, and re-layouts: 4.34 us -> 1.26 us
  Pallas kernels: 12.8 us -> 14.3 us
    unnamed x26 -> x14, local copies, waits for them, and re-layouts: 4.34 us -> 1.26 us
    pallas_call x5, Pallas kernels: 12.8 us -> 14.3 us  [whole(): pl.pallas_call(kernel, out_shape=tuple((jax.ShapeDtypeStruct(s, t) for s,...]
  transfers between devices with their start and end apart: 9 -> 9, of which waited for: 3 -> 3; matrix products, arithmetic and copies ran while one was open for 0% -> 0% of each run, Pallas kernels for 2% -> 3%
where the time goes in v4:
time: 135 us; the launch traced here: 134 us
  blocking collectives  52.8 us (39%)
  starting transfers between devices  40.6 us (30%)
  waiting for transfers between devices  23.9 us (18%)
  Pallas kernels  14.3 us (11%)
    all_gather x1, blocking collectives, on_device(): lax.all_gather(swapped, 'space', axis=0, tiled=True, axis_index_groups=z_...  28.7 us
    all_to_all x2, waiting for transfers between devices, exchange(): lax.all_to_all(x, 'space', split_axis=0, concat_axis=0, tiled=True, axis_...  18.4 us
    all_to_all x2, starting transfers between devices, exchange(): lax.all_to_all(x, 'space', split_axis=0, concat_axis=0, tiled=True, axis_...  16.3 us
    pallas_call x5, Pallas kernels, whole(): pl.pallas_call(kernel, out_shape=tuple((jax.ShapeDtypeStruct(s, t) for s,...  14.3 us
    ppermute x3, starting transfers between devices, along_y(): lax.ppermute(x, 'space', [(place(y, z, c), place(y - step, z, c)) for y,...  12.8 us
    all_gather x2, blocking collectives, of_chip(): lax.all_gather(x, 'space', axis=0, tiled=False, axis_index_groups=chip_gr...  12.6 us
    all_gather x1, blocking collectives, on_device(): cots = lax.all_gather(cots, 'chan', axis=0, tiled=False)  11.5 us
    ppermute x3, starting transfers between devices, along_x(): lax.ppermute(x, 'chan', [(a, (a - step) % chan) for a in range(chan)])  10 us
  transfers between devices with their start and end apart: 9, of which 3 were waited for; matrix products, arithmetic and copies ran while one was open for 0% of the time, Pallas kernels for 3%

profile of v4, /device:TPU:1, one launch (start us, length us, event | category | flops | bytes accessed | tf_op | source)
XLA Modules:
  0.0 134.4 jit_solution(14172290159889485774)
XLA Ops:
  0.6 1.5 %collective-permute-start = (f32[27,4,128]{2,1,0:T(4,128)}, f32[27,4,128]{2,1,0:T(4,128)S(1)}, u32[]{:S(2)}, u32[]{:S(2)}) collective-permute-start(f32[27,4,128]{2,1,0:T(4,128)} %param.8), channel_id=1, source_target_pairs={{0,0},{1,128},{2,256},{3,384},{4,4},{5,132},{6,260},{7,388},{8,8},... | collective-permute-start | bytes 165896 | tf_op jit(solution)/shard_map/ppermute | solution.py:353
  2.1 2.5 %shard_map.86 = f32[328,128]{1,0:T(8,128)} custom-call(s32[27]{0:T(128)} %count_ref.1, f32[128,128]{1,0:T(8,128)} %features_in.1, f32[128,128]{1,0:T(8,128)} %cot_in.1, s32[2,128]{1,0:T(2,128)} %bitcast.20, s32[27,128]{1,0:T(8,128)} %src_in.1, s32[27,128]{1,0:T(8,128)} %dst_in.1), custom_call_target="tpu_custom_call" | custom-call | tf_op jit(solution)/shard_map/pallas_call | solution.py:315
  4.6 8.8 %all-gather.shared_ref.refs_0_ = f32[656,128]{1,0:T(8,128)S(1)} all-gather(f32[328,128]{1,0:T(8,128)} %shard_map.86), channel_id=2, replica_groups={{0,4},{8,12},{16,20},{24,28},{32,36},{40,44},{48,52},{56,60},{64,68},{7..., dimensions={0}, use_global_device_ids=true | all-gather | bytes 503808 | tf_op jit(solution)/shard_map/all_gather | solution.py:351
  13.3 28.7 %all_gather.23.gathered_ref = f32[432,4,128]{2,1,0:T(4,128)S(1)} all-gather(f32[27,4,128]{2,1,0:T(4,128)S(1)} %collective-permute-done), channel_id=1, replica_groups={{0,8,16,24,32,40,48,56,64,72,80,88,96,104,112,120},{4,12,20,28,36,44,52..., dimensions={0}, use_global_device_ids=true | all-gather | bytes 940032 | tf_op jit(solution)/shard_map/all_gather | solution.py:374
  42.0 0.2 shard_map.87.refs_3_
  42.2 7.7 %collective-permute-start.1 = (f32[27,64,128]{2,1,0:T(8,128)S(1)}, f32[27,64,128]{2,1,0:T(8,128)S(1)}, u32[]{:S(2)}, u32[]{:S(2)}) collective-permute-start(f32[27,64,128]{2,1,0:T(8,128)S(1)} %shard_map.87.refs_3_), channel_id=1, source_target_pairs={{0,384},{4,388},{8,392},{12,396},{16,400},{20,404},{24,408},{28,41... | collective-permute-start | bytes 2654216 | tf_op jit(solution)/shard_map/ppermute | solution.py:345
  49.8 2.4 %collective-permute-start.2 = (f32[27,64,128]{2,1,0:T(8,128)S(1)}, f32[27,64,128]{2,1,0:T(8,128)S(1)}, u32[]{:S(2)}, u32[]{:S(2)}) collective-permute-start(f32[27,64,128]{2,1,0:T(8,128)S(1)} %shard_map.87.refs_3_), channel_id=1, source_target_pairs={{0,256},{4,260},{8,264},{12,268},{16,272},{20,276},{24,280},{28,28... | collective-permute-start | bytes 2654216 | tf_op jit(solution)/shard_map/ppermute | solution.py:345
  52.2 2.8 %collective-permute-start.3 = (f32[27,64,128]{2,1,0:T(8,128)S(1)}, f32[27,64,128]{2,1,0:T(8,128)}, u32[]{:S(2)}, u32[]{:S(2)}) collective-permute-start(f32[27,64,128]{2,1,0:T(8,128)S(1)} %shard_map.87.refs_3_), channel_id=1, source_target_pairs={{0,128},{4,132},{8,136},{12,140},{16,144},{20,148},{24,152},{28,15... | collective-permute-start | bytes 2654216 | tf_op jit(solution)/shard_map/ppermute | solution.py:345
  55.0 1.1 shard_map.88
  56.1 8.9 %all-to-all-start = ((f32[64,4,128]{2,1,0:T(4,128)}), f32[64,4,128]{2,1,0:T(4,128)S(1)}, u32[]{:S(2)}, u32[]{:S(2)}) async-start(f32[64,4,128]{2,1,0:T(4,128)} %bitcast.1), calls=%async_computation | async-start | bytes 262144 | tf_op jit(solution)/shard_map/all_to_all | solution.py:389
  65.0 11.5 %all-gather.1 = f32[1024,128]{1,0:T(8,128)} all-gather(f32[256,128]{1,0:T(8,128)S(1)} %get-tuple-element.22), channel_id=3, replica_groups=mesh['space'=128,'chan'=4] {'chan'}, dimensions={0}, use_global_device_ids=true | all-gather | bytes 655360 | tf_op jit(solution)/shard_map/all_gather | solution.py:385
  76.6 18.4 %all-to-all-done = f32[64,4,128]{2,1,0:T(4,128)S(1)} async-done(((f32[64,4,128]{2,1,0:T(4,128)}), f32[64,4,128]{2,1,0:T(4,128)S(1)}, u32[]{:S(2)}, u32[]{:S(2)}) %all-to-all-start) | async-done | bytes 131104 | tf_op jit(solution)/shard_map/all_to_all | solution.py:389
  95.0 0.9 copy-done.4
  96.0 0.3 copy-done.5
  96.3 9.7 %shard_map.89 = (f32[256,128]{1,0:T(8,128)}, f32[128,128]{1,0:T(8,128)}, f32[256,128]{1,0:T(8,128)}, f32[256,128]{1,0:T(8,128)}, f32[256,128]{1,0:T(8,128)}, /*index=5*/f32[256,128]{1,0:T(8,128)}) custom-call(f32[656,128]{1,0:T(8,128)} %copy-done.1, f32[256,128]{1,0:T(8,128)} %bitcast.18, f32[4,256,128]{2,1,0:T(8,128)} %bitcast.16, f32[27,64,128]{2,1,0:T(8,128)} %copy-done, ...), custom_call_target="tpu_custom_call" | custom-call | tf_op jit(solution)/shard_map/pallas_call | solution.py:315
  106.0 7.4 %all-to-all-start.1 = ((f32[64,4,128]{2,1,0:T(4,128)}), f32[64,4,128]{2,1,0:T(4,128)S(1)}, u32[]{:S(2)}, u32[]{:S(2)}) async-start(f32[64,4,128]{2,1,0:T(4,128)} %bitcast.19), calls=%async_computation.1 | async-start | bytes 262144 | tf_op jit(solution)/shard_map/all_to_all | solution.py:389
  113.4 3.6 %collective-permute-start.4 = (f32[256,128]{1,0:T(8,128)}, f32[256,128]{1,0:T(8,128)S(1)}, u32[]{:S(2)}, u32[]{:S(2)}) collective-permute-start(f32[256,128]{1,0:T(8,128)} %get-tuple-element.28), channel_id=1, source_target_pairs={{0,2},{1,3},{2,0},{3,1},{4,6},{5,7},{6,4},{7,5},{8,10},{9,11},{10,... | collective-permute-start | bytes 393224 | tf_op jit(solution)/shard_map/ppermute | solution.py:348
  117.1 4.5 %collective-permute-start.5 = (f32[256,128]{1,0:T(8,128)}, f32[256,128]{1,0:T(8,128)S(1)}, u32[]{:S(2)}, u32[]{:S(2)}) collective-permute-start(f32[256,128]{1,0:T(8,128)} %get-tuple-element.29), channel_id=1, source_target_pairs={{0,3},{1,0},{2,1},{3,2},{4,7},{5,4},{6,5},{7,6},{8,11},{9,8},{10,9... | collective-permute-start | bytes 393224 | tf_op jit(solution)/shard_map/ppermute | solution.py:348
  121.5 1.9 %collective-permute-start.6 = (f32[256,128]{1,0:T(8,128)}, f32[256,128]{1,0:T(8,128)S(1)}, u32[]{:S(2)}, u32[]{:S(2)}) collective-permute-start(f32[256,128]{1,0:T(8,128)} %get-tuple-element.30), channel_id=1, source_target_pairs={{0,1},{1,2},{2,3},{3,0},{4,5},{5,6},{6,7},{7,4},{8,9},{9,10},{10,1... | collective-permute-start | bytes 393224 | tf_op jit(solution)/shard_map/ppermute | solution.py:348
  123.5 1.7 %collective-permute-done.5.refs_2_ = f32[256,128]{1,0:T(8,128)S(1)} collective-permute-done((f32[256,128]{1,0:T(8,128)}, f32[256,128]{1,0:T(8,128)S(1)}, u32[]{:S(2)}, u32[]{:S(2)}) %collective-permute-start.5) | collective-permute-done | bytes 131104 | tf_op jit(solution)/shard_map/ppermute | solution.py:348
  125.2 3.7 %collective-permute-done.6.refs_3_ = f32[256,128]{1,0:T(8,128)S(1)} collective-permute-done((f32[256,128]{1,0:T(8,128)}, f32[256,128]{1,0:T(8,128)S(1)}, u32[]{:S(2)}, u32[]{:S(2)}) %collective-permute-start.6) | collective-permute-done | bytes 131104 | tf_op jit(solution)/shard_map/ppermute | solution.py:348
  129.0 0.9 shard_map.90
  129.9 3.8 %all-gather.2 = f32[512,128]{1,0:T(8,128)S(1)} all-gather(f32[256,128]{1,0:T(8,128)S(1)} %get-tuple-element.32), channel_id=4, replica_groups={{0,4},{8,12},{16,20},{24,28},{32,36},{40,44},{48,52},{56,60},{64,68},{7..., dimensions={0}, use_global_device_ids=true | all-gather | bytes 393216 | tf_op jit(solution)/shard_map/all_gather | solution.py:351
  133.7 0.7 fusion
  (18 shorter events, 0.0 us)
Async XLA Ops:
  0.6 12.7 %collective-permute-start = (f32[27,4,128]{2,1,0:T(4,128)}, f32[27,4,128]{2,1,0:T(4,128)S(1)}, u32[]{:S(2)}, u32[]{:S(2)}) collective-permute-start(f32[27,4,128]{2,1,0:T(4,128)} %param.8), channel_id=1, source_target_pairs={{0,0},{1,128},{2,256},{3,384},{4,4},{5,132},{6,260},{7,388},{8,8},... | collective-permute-start | bytes 165896 | tf_op jit(solution)/shard_map/ppermute | solution.py:353
  13.3 41.6 %copy-start.1 = (f32[656,128]{1,0:T(8,128)}, f32[656,128]{1,0:T(8,128)S(1)}, u32[]{:S(2)}) copy-start(f32[656,128]{1,0:T(8,128)S(1)} %all-gather.shared_ref.refs_0_) | copy-start | bytes 1007620
  42.2 54.1 %copy-start = (f32[27,64,128]{2,1,0:T(8,128)}, f32[27,64,128]{2,1,0:T(8,128)S(1)}, u32[]{:S(2)}) copy-start(f32[27,64,128]{2,1,0:T(8,128)S(1)} %shard_map.87.refs_3_) | copy-start | bytes 2654212
  42.2 52.8 %collective-permute-start.1 = (f32[27,64,128]{2,1,0:T(8,128)S(1)}, f32[27,64,128]{2,1,0:T(8,128)S(1)}, u32[]{:S(2)}, u32[]{:S(2)}) collective-permute-start(f32[27,64,128]{2,1,0:T(8,128)S(1)} %shard_map.87.refs_3_), channel_id=1, source_target_pairs={{0,384},{4,388},{8,392},{12,396},{16,400},{20,404},{24,408},{28,41... | collective-permute-start | bytes 2654216 | tf_op jit(solution)/shard_map/ppermute | solution.py:345
  49.8 45.2 %collective-permute-start.2 = (f32[27,64,128]{2,1,0:T(8,128)S(1)}, f32[27,64,128]{2,1,0:T(8,128)S(1)}, u32[]{:S(2)}, u32[]{:S(2)}) collective-permute-start(f32[27,64,128]{2,1,0:T(8,128)S(1)} %shard_map.87.refs_3_), channel_id=1, source_target_pairs={{0,256},{4,260},{8,264},{12,268},{16,272},{20,276},{24,280},{28,28... | collective-permute-start | bytes 2654216 | tf_op jit(solution)/shard_map/ppermute | solution.py:345
  52.2 42.8 %collective-permute-start.3 = (f32[27,64,128]{2,1,0:T(8,128)S(1)}, f32[27,64,128]{2,1,0:T(8,128)}, u32[]{:S(2)}, u32[]{:S(2)}) collective-permute-start(f32[27,64,128]{2,1,0:T(8,128)S(1)} %shard_map.87.refs_3_), channel_id=1, source_target_pairs={{0,128},{4,132},{8,136},{12,140},{16,144},{20,148},{24,152},{28,15... | collective-permute-start | bytes 2654216 | tf_op jit(solution)/shard_map/ppermute | solution.py:345
  56.1 38.9 %all-to-all-start = ((f32[64,4,128]{2,1,0:T(4,128)}), f32[64,4,128]{2,1,0:T(4,128)S(1)}, u32[]{:S(2)}, u32[]{:S(2)}) async-start(f32[64,4,128]{2,1,0:T(4,128)} %bitcast.1), calls=%async_computation | async-start | bytes 262144 | tf_op jit(solution)/shard_map/all_to_all | solution.py:389
  95.0 0.9 copy-start.6
  95.0 0.9 copy-start.4
  95.0 1.3 copy-start.5
  106.0 22.9 %copy-start.2 = (f32[256,128]{1,0:T(8,128)S(1)}, f32[256,128]{1,0:T(8,128)}, u32[]{:S(2)}) copy-start(f32[256,128]{1,0:T(8,128)} %get-tuple-element.27.refs_0_) | copy-start | bytes 393220
  106.0 22.9 %copy-start.3 = (f32[128,128]{1,0:T(8,128)S(1)}, f32[128,128]{1,0:T(8,128)}, u32[]{:S(2)}) copy-start(f32[128,128]{1,0:T(8,128)} %get-tuple-element.24.local_ref) | copy-start | bytes 196612
  106.0 22.9 %all-to-all-start.1 = ((f32[64,4,128]{2,1,0:T(4,128)}), f32[64,4,128]{2,1,0:T(4,128)S(1)}, u32[]{:S(2)}, u32[]{:S(2)}) async-start(f32[64,4,128]{2,1,0:T(4,128)} %bitcast.19), calls=%async_computation.1 | async-start | bytes 262144 | tf_op jit(solution)/shard_map/all_to_all | solution.py:389
  113.4 10.0 %collective-permute-start.4 = (f32[256,128]{1,0:T(8,128)}, f32[256,128]{1,0:T(8,128)S(1)}, u32[]{:S(2)}, u32[]{:S(2)}) collective-permute-start(f32[256,128]{1,0:T(8,128)} %get-tuple-element.28), channel_id=1, source_target_pairs={{0,2},{1,3},{2,0},{3,1},{4,6},{5,7},{6,4},{7,5},{8,10},{9,11},{10,... | collective-permute-start | bytes 393224 | tf_op jit(solution)/shard_map/ppermute | solution.py:348
  117.1 8.2 %collective-permute-start.5 = (f32[256,128]{1,0:T(8,128)}, f32[256,128]{1,0:T(8,128)S(1)}, u32[]{:S(2)}, u32[]{:S(2)}) collective-permute-start(f32[256,128]{1,0:T(8,128)} %get-tuple-element.29), channel_id=1, source_target_pairs={{0,3},{1,0},{2,1},{3,2},{4,7},{5,4},{6,5},{7,6},{8,11},{9,8},{10,9... | collective-permute-start | bytes 393224 | tf_op jit(solution)/shard_map/ppermute | solution.py:348
  121.5 7.4 %collective-permute-start.6 = (f32[256,128]{1,0:T(8,128)}, f32[256,128]{1,0:T(8,128)S(1)}, u32[]{:S(2)}, u32[]{:S(2)}) collective-permute-start(f32[256,128]{1,0:T(8,128)} %get-tuple-element.30), channel_id=1, source_target_pairs={{0,1},{1,2},{2,3},{3,0},{4,5},{5,6},{6,7},{7,4},{8,9},{9,10},{10,1... | collective-permute-start | bytes 393224 | tf_op jit(solution)/shard_map/ppermute | solution.py:348

commit v5 on v4

--- a/solution.py
+++ b/solution.py
@@ -23,13 +23,6 @@
     return high, (x - high.astype(F32)).astype(BF16)
 
 
-def split3(x):
-    high = x.astype(BF16)
-    rest = x - high.astype(F32)
-    middle = rest.astype(BF16)
-    return high, middle, (rest - middle.astype(F32)).astype(BF16)
-
-
 def dot(a, b):
     return jnp.dot(a, b, preferred_element_type=F32)
 
@@ -51,13 +44,13 @@
 
 
 def pick_left(onehot, x):
-    a, b, c = split3(x)
-    return (dot(onehot, a) + dot(onehot, b)) + dot(onehot, c)
+    high, low = split2(x)
+    return dot(onehot, high) + dot(onehot, low)
 
 
 def pick_right(x, onehot):
-    a, b, c = split3(x)
-    return (dot(a, onehot) + dot(b, onehot)) + dot(c, onehot)
+    high, low = split2(x)
+    return dot(high, onehot) + dot(low, onehot)
 
 
 def to_inner(n):
@@ -122,16 +115,16 @@
         base = device * SHARED
         cot_ref[device * rows : (device + 1) * rows, :] = shared_ref[base : base + rows, :]
         inner = shared_ref[base + FEATURES : base + FEATURES + rows, :]
-        parts = split3(pltpu.roll(inner, half * core_index(), axis=1))
+        parts = split2(pltpu.roll(inner, half * core_index(), axis=1))
         for slot in range(slots):
             line = shared_ref[base + SENDS + slot : base + SENDS + slot + 1, :]
             sends_ref[device * slots + slot : device * slots + slot + 1, :] = line
             onehot = onehot_rows(line, rows)
-            a, b, c = (
+            high, low = (
                 lax.dot_general(onehot, part, (((0,), (0,)), ((), ())), preferred_element_type=F32)
                 for part in parts
             )
-            picked_ref[...] = (a + b) + c
+            picked_ref[...] = high + low
             both = [picked_ref[pl.ds(d, chips, stride=CORES), :][:, :half] for d in range(CORES)]
             outgoing_ref[pl.ds(device * slots + slot, chips, stride=CORES * slots), :] = jnp.concatenate(
                 both, axis=1

time: 135 us -> 135 us (level)
  no operation moved by 1% of the time
where the time goes in v5:
time: 135 us; the launch traced here: 134 us
  blocking collectives  52.8 us (39%)
  starting transfers between devices  40.8 us (30%)
  waiting for transfers between devices  23.8 us (18%)
  Pallas kernels  14.2 us (11%)
    all_gather x1, blocking collectives, on_device(): lax.all_gather(swapped, 'space', axis=0, tiled=True, axis_index_groups=z_...  28.7 us
    all_to_all x2, waiting for transfers between devices, exchange(): lax.all_to_all(x, 'space', split_axis=0, concat_axis=0, tiled=True, axis_...  18.3 us
    all_to_all x2, starting transfers between devices, exchange(): lax.all_to_all(x, 'space', split_axis=0, concat_axis=0, tiled=True, axis_...  16.5 us
    pallas_call x5, Pallas kernels, whole(): pl.pallas_call(kernel, out_shape=tuple((jax.ShapeDtypeStruct(s, t) for s,...  14.2 us
    ppermute x3, starting transfers between devices, along_y(): lax.ppermute(x, 'space', [(place(y, z, c), place(y - step, z, c)) for y,...  12.8 us
    all_gather x2, blocking collectives, of_chip(): lax.all_gather(x, 'space', axis=0, tiled=False, axis_index_groups=chip_gr...  12.6 us
    all_gather x1, blocking collectives, on_device(): cots = lax.all_gather(cots, 'chan', axis=0, tiled=False)  11.5 us
    ppermute x3, starting transfers between devices, along_x(): lax.ppermute(x, 'chan', [(a, (a - step) % chan) for a in range(chan)])  10.1 us
  transfers between devices with their start and end apart: 9, of which 3 were waited for; matrix products, arithmetic and copies ran while one was open for 0% of the time, Pallas kernels for 3%

profile of v5, /device:TPU:1, one launch (start us, length us, event | category | flops | bytes accessed | tf_op | source)
XLA Modules:
  0.0 134.3 jit_solution(6263951478807156872)
XLA Ops:
  0.6 1.5 %collective-permute-start = (f32[27,4,128]{2,1,0:T(4,128)}, f32[27,4,128]{2,1,0:T(4,128)S(1)}, u32[]{:S(2)}, u32[]{:S(2)}) collective-permute-start(f32[27,4,128]{2,1,0:T(4,128)} %param.8), channel_id=1, source_target_pairs={{0,0},{1,128},{2,256},{3,384},{4,4},{5,132},{6,260},{7,388},{8,8},... | collective-permute-start | bytes 165896 | tf_op jit(solution)/shard_map/ppermute | solution.py:346
  2.1 2.5 %shard_map.86 = f32[328,128]{1,0:T(8,128)} custom-call(s32[27]{0:T(128)} %count_ref.1, f32[128,128]{1,0:T(8,128)} %features_in.1, f32[128,128]{1,0:T(8,128)} %cot_in.1, s32[2,128]{1,0:T(2,128)} %bitcast.20, s32[27,128]{1,0:T(8,128)} %src_in.1, s32[27,128]{1,0:T(8,128)} %dst_in.1), custom_call_target="tpu_custom_call" | custom-call | tf_op jit(solution)/shard_map/pallas_call | solution.py:308
  4.6 8.8 %all-gather.shared_ref.refs_0_ = f32[656,128]{1,0:T(8,128)S(1)} all-gather(f32[328,128]{1,0:T(8,128)} %shard_map.86), channel_id=2, replica_groups={{0,4},{8,12},{16,20},{24,28},{32,36},{40,44},{48,52},{56,60},{64,68},{7..., dimensions={0}, use_global_device_ids=true | all-gather | bytes 503808 | tf_op jit(solution)/shard_map/all_gather | solution.py:344
  13.3 28.7 %all_gather.23.gathered_ref = f32[432,4,128]{2,1,0:T(4,128)S(1)} all-gather(f32[27,4,128]{2,1,0:T(4,128)S(1)} %collective-permute-done), channel_id=1, replica_groups={{0,8,16,24,32,40,48,56,64,72,80,88,96,104,112,120},{4,12,20,28,36,44,52..., dimensions={0}, use_global_device_ids=true | all-gather | bytes 940032 | tf_op jit(solution)/shard_map/all_gather | solution.py:367
  42.0 0.2 shard_map.87.refs_3_
  42.2 7.6 %collective-permute-start.1 = (f32[27,64,128]{2,1,0:T(8,128)S(1)}, f32[27,64,128]{2,1,0:T(8,128)S(1)}, u32[]{:S(2)}, u32[]{:S(2)}) collective-permute-start(f32[27,64,128]{2,1,0:T(8,128)S(1)} %shard_map.87.refs_3_), channel_id=1, source_target_pairs={{0,384},{4,388},{8,392},{12,396},{16,400},{20,404},{24,408},{28,41... | collective-permute-start | bytes 2654216 | tf_op jit(solution)/shard_map/ppermute | solution.py:338
  49.8 2.4 %collective-permute-start.2 = (f32[27,64,128]{2,1,0:T(8,128)S(1)}, f32[27,64,128]{2,1,0:T(8,128)S(1)}, u32[]{:S(2)}, u32[]{:S(2)}) collective-permute-start(f32[27,64,128]{2,1,0:T(8,128)S(1)} %shard_map.87.refs_3_), channel_id=1, source_target_pairs={{0,256},{4,260},{8,264},{12,268},{16,272},{20,276},{24,280},{28,28... | collective-permute-start | bytes 2654216 | tf_op jit(solution)/shard_map/ppermute | solution.py:338
  52.2 2.8 %collective-permute-start.3 = (f32[27,64,128]{2,1,0:T(8,128)S(1)}, f32[27,64,128]{2,1,0:T(8,128)}, u32[]{:S(2)}, u32[]{:S(2)}) collective-permute-start(f32[27,64,128]{2,1,0:T(8,128)S(1)} %shard_map.87.refs_3_), channel_id=1, source_target_pairs={{0,128},{4,132},{8,136},{12,140},{16,144},{20,148},{24,152},{28,15... | collective-permute-start | bytes 2654216 | tf_op jit(solution)/shard_map/ppermute | solution.py:338
  55.0 1.1 shard_map.88
  56.0 9.0 %all-to-all-start = ((f32[64,4,128]{2,1,0:T(4,128)}), f32[64,4,128]{2,1,0:T(4,128)S(1)}, u32[]{:S(2)}, u32[]{:S(2)}) async-start(f32[64,4,128]{2,1,0:T(4,128)} %bitcast.1), calls=%async_computation | async-start | bytes 262144 | tf_op jit(solution)/shard_map/all_to_all | solution.py:382
  65.1 11.5 %all-gather.1 = f32[1024,128]{1,0:T(8,128)} all-gather(f32[256,128]{1,0:T(8,128)S(1)} %get-tuple-element.22), channel_id=3, replica_groups=mesh['space'=128,'chan'=4] {'chan'}, dimensions={0}, use_global_device_ids=true | all-gather | bytes 655360 | tf_op jit(solution)/shard_map/all_gather | solution.py:378
  76.6 18.3 %all-to-all-done = f32[64,4,128]{2,1,0:T(4,128)S(1)} async-done(((f32[64,4,128]{2,1,0:T(4,128)}), f32[64,4,128]{2,1,0:T(4,128)S(1)}, u32[]{:S(2)}, u32[]{:S(2)}) %all-to-all-start) | async-done | bytes 131104 | tf_op jit(solution)/shard_map/all_to_all | solution.py:382
  94.9 0.9 copy-done.4
  95.8 0.3 copy-done.5
  96.2 9.7 %shard_map.89 = (f32[256,128]{1,0:T(8,128)}, f32[128,128]{1,0:T(8,128)}, f32[256,128]{1,0:T(8,128)}, f32[256,128]{1,0:T(8,128)}, f32[256,128]{1,0:T(8,128)}, /*index=5*/f32[256,128]{1,0:T(8,128)}) custom-call(f32[656,128]{1,0:T(8,128)} %copy-done.1, f32[256,128]{1,0:T(8,128)} %bitcast.18, f32[4,256,128]{2,1,0:T(8,128)} %bitcast.16, f32[27,64,128]{2,1,0:T(8,128)} %copy-done, ...), custom_call_target="tpu_custom_call" | custom-call | tf_op jit(solution)/shard_map/pallas_call | solution.py:308
  105.9 7.5 %all-to-all-start.1 = ((f32[64,4,128]{2,1,0:T(4,128)}), f32[64,4,128]{2,1,0:T(4,128)S(1)}, u32[]{:S(2)}, u32[]{:S(2)}) async-start(f32[64,4,128]{2,1,0:T(4,128)} %bitcast.19), calls=%async_computation.1 | async-start | bytes 262144 | tf_op jit(solution)/shard_map/all_to_all | solution.py:382
  113.4 3.6 %collective-permute-start.4 = (f32[256,128]{1,0:T(8,128)}, f32[256,128]{1,0:T(8,128)S(1)}, u32[]{:S(2)}, u32[]{:S(2)}) collective-permute-start(f32[256,128]{1,0:T(8,128)} %get-tuple-element.28), channel_id=1, source_target_pairs={{0,2},{1,3},{2,0},{3,1},{4,6},{5,7},{6,4},{7,5},{8,10},{9,11},{10,... | collective-permute-start | bytes 393224 | tf_op jit(solution)/shard_map/ppermute | solution.py:341
  117.1 4.5 %collective-permute-start.5 = (f32[256,128]{1,0:T(8,128)}, f32[256,128]{1,0:T(8,128)S(1)}, u32[]{:S(2)}, u32[]{:S(2)}) collective-permute-start(f32[256,128]{1,0:T(8,128)} %get-tuple-element.29), channel_id=1, source_target_pairs={{0,3},{1,0},{2,1},{3,2},{4,7},{5,4},{6,5},{7,6},{8,11},{9,8},{10,9... | collective-permute-start | bytes 393224 | tf_op jit(solution)/shard_map/ppermute | solution.py:341
  121.6 1.9 %collective-permute-start.6 = (f32[256,128]{1,0:T(8,128)}, f32[256,128]{1,0:T(8,128)S(1)}, u32[]{:S(2)}, u32[]{:S(2)}) collective-permute-start(f32[256,128]{1,0:T(8,128)} %get-tuple-element.30), channel_id=1, source_target_pairs={{0,1},{1,2},{2,3},{3,0},{4,5},{5,6},{6,7},{7,4},{8,9},{9,10},{10,1... | collective-permute-start | bytes 393224 | tf_op jit(solution)/shard_map/ppermute | solution.py:341
  123.5 1.7 %collective-permute-done.5.refs_2_ = f32[256,128]{1,0:T(8,128)S(1)} collective-permute-done((f32[256,128]{1,0:T(8,128)}, f32[256,128]{1,0:T(8,128)S(1)}, u32[]{:S(2)}, u32[]{:S(2)}) %collective-permute-start.5) | collective-permute-done | bytes 131104 | tf_op jit(solution)/shard_map/ppermute | solution.py:341
  125.2 3.8 %collective-permute-done.6.refs_3_ = f32[256,128]{1,0:T(8,128)S(1)} collective-permute-done((f32[256,128]{1,0:T(8,128)}, f32[256,128]{1,0:T(8,128)S(1)}, u32[]{:S(2)}, u32[]{:S(2)}) %collective-permute-start.6) | collective-permute-done | bytes 131104 | tf_op jit(solution)/shard_map/ppermute | solution.py:341
  129.0 0.8 shard_map.90
  129.8 3.8 %all-gather.2 = f32[512,128]{1,0:T(8,128)S(1)} all-gather(f32[256,128]{1,0:T(8,128)S(1)} %get-tuple-element.32), channel_id=4, replica_groups={{0,4},{8,12},{16,20},{24,28},{32,36},{40,44},{48,52},{56,60},{64,68},{7..., dimensions={0}, use_global_device_ids=true | all-gather | bytes 393216 | tf_op jit(solution)/shard_map/all_gather | solution.py:344
  133.6 0.7 fusion
  (18 shorter events, 0.0 us)
Async XLA Ops:
  0.6 12.7 %collective-permute-start = (f32[27,4,128]{2,1,0:T(4,128)}, f32[27,4,128]{2,1,0:T(4,128)S(1)}, u32[]{:S(2)}, u32[]{:S(2)}) collective-permute-start(f32[27,4,128]{2,1,0:T(4,128)} %param.8), channel_id=1, source_target_pairs={{0,0},{1,128},{2,256},{3,384},{4,4},{5,132},{6,260},{7,388},{8,8},... | collective-permute-start | bytes 165896 | tf_op jit(solution)/shard_map/ppermute | solution.py:346
  13.3 41.6 %copy-start.1 = (f32[656,128]{1,0:T(8,128)}, f32[656,128]{1,0:T(8,128)S(1)}, u32[]{:S(2)}) copy-start(f32[656,128]{1,0:T(8,128)S(1)} %all-gather.shared_ref.refs_0_) | copy-start | bytes 1007620
  42.2 54.0 %copy-start = (f32[27,64,128]{2,1,0:T(8,128)}, f32[27,64,128]{2,1,0:T(8,128)S(1)}, u32[]{:S(2)}) copy-start(f32[27,64,128]{2,1,0:T(8,128)S(1)} %shard_map.87.refs_3_) | copy-start | bytes 2654212
  42.2 52.7 %collective-permute-start.1 = (f32[27,64,128]{2,1,0:T(8,128)S(1)}, f32[27,64,128]{2,1,0:T(8,128)S(1)}, u32[]{:S(2)}, u32[]{:S(2)}) collective-permute-start(f32[27,64,128]{2,1,0:T(8,128)S(1)} %shard_map.87.refs_3_), channel_id=1, source_target_pairs={{0,384},{4,388},{8,392},{12,396},{16,400},{20,404},{24,408},{28,41... | collective-permute-start | bytes 2654216 | tf_op jit(solution)/shard_map/ppermute | solution.py:338
  49.8 45.1 %collective-permute-start.2 = (f32[27,64,128]{2,1,0:T(8,128)S(1)}, f32[27,64,128]{2,1,0:T(8,128)S(1)}, u32[]{:S(2)}, u32[]{:S(2)}) collective-permute-start(f32[27,64,128]{2,1,0:T(8,128)S(1)} %shard_map.87.refs_3_), channel_id=1, source_target_pairs={{0,256},{4,260},{8,264},{12,268},{16,272},{20,276},{24,280},{28,28... | collective-permute-start | bytes 2654216 | tf_op jit(solution)/shard_map/ppermute | solution.py:338
  52.2 42.7 %collective-permute-start.3 = (f32[27,64,128]{2,1,0:T(8,128)S(1)}, f32[27,64,128]{2,1,0:T(8,128)}, u32[]{:S(2)}, u32[]{:S(2)}) collective-permute-start(f32[27,64,128]{2,1,0:T(8,128)S(1)} %shard_map.87.refs_3_), channel_id=1, source_target_pairs={{0,128},{4,132},{8,136},{12,140},{16,144},{20,148},{24,152},{28,15... | collective-permute-start | bytes 2654216 | tf_op jit(solution)/shard_map/ppermute | solution.py:338
  56.0 38.8 %all-to-all-start = ((f32[64,4,128]{2,1,0:T(4,128)}), f32[64,4,128]{2,1,0:T(4,128)S(1)}, u32[]{:S(2)}, u32[]{:S(2)}) async-start(f32[64,4,128]{2,1,0:T(4,128)} %bitcast.1), calls=%async_computation | async-start | bytes 262144 | tf_op jit(solution)/shard_map/all_to_all | solution.py:382
  94.9 0.9 copy-start.6
  94.9 0.9 copy-start.4
  94.9 1.3 copy-start.5
  105.9 23.1 %copy-start.2 = (f32[256,128]{1,0:T(8,128)S(1)}, f32[256,128]{1,0:T(8,128)}, u32[]{:S(2)}) copy-start(f32[256,128]{1,0:T(8,128)} %get-tuple-element.27.refs_0_) | copy-start | bytes 393220
  105.9 23.1 %copy-start.3 = (f32[128,128]{1,0:T(8,128)S(1)}, f32[128,128]{1,0:T(8,128)}, u32[]{:S(2)}) copy-start(f32[128,128]{1,0:T(8,128)} %get-tuple-element.24.local_ref) | copy-start | bytes 196612
  105.9 23.1 %all-to-all-start.1 = ((f32[64,4,128]{2,1,0:T(4,128)}), f32[64,4,128]{2,1,0:T(4,128)S(1)}, u32[]{:S(2)}, u32[]{:S(2)}) async-start(f32[64,4,128]{2,1,0:T(4,128)} %bitcast.19), calls=%async_computation.1 | async-start | bytes 262144 | tf_op jit(solution)/shard_map/all_to_all | solution.py:382
  113.4 10.1 %collective-permute-start.4 = (f32[256,128]{1,0:T(8,128)}, f32[256,128]{1,0:T(8,128)S(1)}, u32[]{:S(2)}, u32[]{:S(2)}) collective-permute-start(f32[256,128]{1,0:T(8,128)} %get-tuple-element.28), channel_id=1, source_target_pairs={{0,2},{1,3},{2,0},{3,1},{4,6},{5,7},{6,4},{7,5},{8,10},{9,11},{10,... | collective-permute-start | bytes 393224 | tf_op jit(solution)/shard_map/ppermute | solution.py:341
  117.1 8.2 %collective-permute-start.5 = (f32[256,128]{1,0:T(8,128)}, f32[256,128]{1,0:T(8,128)S(1)}, u32[]{:S(2)}, u32[]{:S(2)}) collective-permute-start(f32[256,128]{1,0:T(8,128)} %get-tuple-element.29), channel_id=1, source_target_pairs={{0,3},{1,0},{2,1},{3,2},{4,7},{5,4},{6,5},{7,6},{8,11},{9,8},{10,9... | collective-permute-start | bytes 393224 | tf_op jit(solution)/shard_map/ppermute | solution.py:341
  121.6 7.4 %collective-permute-start.6 = (f32[256,128]{1,0:T(8,128)}, f32[256,128]{1,0:T(8,128)S(1)}, u32[]{:S(2)}, u32[]{:S(2)}) collective-permute-start(f32[256,128]{1,0:T(8,128)} %get-tuple-element.30), channel_id=1, source_target_pairs={{0,1},{1,2},{2,3},{3,0},{4,5},{5,6},{6,7},{7,4},{8,9},{9,10},{10,1... | collective-permute-start | bytes 393224 | tf_op jit(solution)/shard_map/ppermute | solution.py:341

commit v6 on v4

--- a/solution.py
+++ b/solution.py
@@ -370,11 +370,6 @@
         mebibytes=LARGE,
     )
     shared = of_chip(shared).reshape(CORES * SHARED, width)
-    swapped, shared = lax.optimization_barrier((swapped, shared))
-    gathered = lax.all_gather(swapped, "space", axis=0, tiled=True, axis_index_groups=z_groups)
-    (own,) = whole(regroup_kernel, [((offsets, 4 * nz, width), F32)], (gathered,), mebibytes=SMALL)
-    shared, own = lax.optimization_barrier((shared, own))
-    pieces = [own] + [along_y(own, s) for s in (1, 2, 3)]
     outgoing, cots, sends = whole(
         outgoing_kernel,
         [((halo_rows, width), F32), ((CORES * rows, width), F32), ((CORES * slots, peers), F32)],
@@ -382,6 +377,11 @@
         scratch=[pltpu.VMEM((peers, width), F32)],
         mebibytes=SMALL,
     )
+    swapped, shared, outgoing, cots = lax.optimization_barrier((swapped, shared, outgoing, cots))
+    gathered = lax.all_gather(swapped, "space", axis=0, tiled=True, axis_index_groups=z_groups)
+    (own,) = whole(regroup_kernel, [((offsets, 4 * nz, width), F32)], (gathered,), mebibytes=SMALL)
+    shared, outgoing, cots, own = lax.optimization_barrier((shared, outgoing, cots, own))
+    pieces = [own] + [along_y(own, s) for s in (1, 2, 3)]
     cots = lax.all_gather(cots, "chan", axis=0, tiled=False)
 
     def exchange(x):

time: 135 us -> 136 us (level)
  no operation moved by 1% of the time
where the time goes in v6:
time: 136 us; the launch traced here: 135 us
  blocking collectives  53.1 us (39%)
  starting transfers between devices  39.7 us (29%)
  waiting for transfers between devices  25.1 us (18%)
  Pallas kernels  14.3 us (11%)
    all_gather x1, blocking collectives, on_device(): lax.all_gather(swapped, 'space', axis=0, tiled=True, axis_index_groups=z_...  28.7 us
    all_to_all x2, waiting for transfers between devices, exchange(): lax.all_to_all(x, 'space', split_axis=0, concat_axis=0, tiled=True, axis_...  19.6 us
    all_to_all x2, starting transfers between devices, exchange(): lax.all_to_all(x, 'space', split_axis=0, concat_axis=0, tiled=True, axis_...  16.1 us
    pallas_call x5, Pallas kernels, whole(): pl.pallas_call(kernel, out_shape=tuple((jax.ShapeDtypeStruct(s, t) for s,...  14.3 us
    ppermute x3, starting transfers between devices, along_y(): lax.ppermute(x, 'space', [(place(y, z, c), place(y - step, z, c)) for y,...  12.7 us
    all_gather x2, blocking collectives, of_chip(): lax.all_gather(x, 'space', axis=0, tiled=False, axis_index_groups=chip_gr...  12.6 us
    all_gather x1, blocking collectives, on_device(): cots = lax.all_gather(cots, 'chan', axis=0, tiled=False)  11.8 us
    ppermute x3, starting transfers between devices, along_x(): lax.ppermute(x, 'chan', [(a, (a - step) % chan) for a in range(chan)])  9.43 us
  transfers between devices with their start and end apart: 9, of which 3 were waited for; matrix products, arithmetic and copies ran while one was open for 0% of the time, Pallas kernels for 3%

profile of v6, /device:TPU:1, one launch (start us, length us, event | category | flops | bytes accessed | tf_op | source)
XLA Modules:
  0.0 134.9 jit_solution(2282360688613342702)
XLA Ops:
  0.6 1.5 %collective-permute-start = (f32[27,4,128]{2,1,0:T(4,128)}, f32[27,4,128]{2,1,0:T(4,128)S(1)}, u32[]{:S(2)}, u32[]{:S(2)}) collective-permute-start(f32[27,4,128]{2,1,0:T(4,128)} %param.8), channel_id=1, source_target_pairs={{0,0},{1,128},{2,256},{3,384},{4,4},{5,132},{6,260},{7,388},{8,8},... | collective-permute-start | bytes 165896 | tf_op jit(solution)/shard_map/ppermute | solution.py:353
  2.1 2.5 %shard_map.86 = f32[328,128]{1,0:T(8,128)} custom-call(s32[27]{0:T(128)} %count_ref.1, f32[128,128]{1,0:T(8,128)} %features_in.1, f32[128,128]{1,0:T(8,128)} %cot_in.1, s32[2,128]{1,0:T(2,128)} %bitcast.20, s32[27,128]{1,0:T(8,128)} %src_in.1, s32[27,128]{1,0:T(8,128)} %dst_in.1), custom_call_target="tpu_custom_call" | custom-call | tf_op jit(solution)/shard_map/pallas_call | solution.py:315
  4.6 8.8 %all-gather.shared_ref.refs_0_ = f32[656,128]{1,0:T(8,128)S(1)} all-gather(f32[328,128]{1,0:T(8,128)} %shard_map.86), channel_id=2, replica_groups={{0,4},{8,12},{16,20},{24,28},{32,36},{40,44},{48,52},{56,60},{64,68},{7..., dimensions={0}, use_global_device_ids=true | all-gather | bytes 503808 | tf_op jit(solution)/shard_map/all_gather | solution.py:351
  13.3 1.1 shard_map.87
  14.4 28.7 %all_gather.23.gathered_ref = f32[432,4,128]{2,1,0:T(4,128)S(1)} all-gather(f32[27,4,128]{2,1,0:T(4,128)S(1)} %collective-permute-done), channel_id=1, replica_groups={{0,8,16,24,32,40,48,56,64,72,80,88,96,104,112,120},{4,12,20,28,36,44,52..., dimensions={0}, use_global_device_ids=true | all-gather | bytes 940032 | tf_op jit(solution)/shard_map/all_gather | solution.py:381
  43.1 0.2 shard_map.88.refs_3_
  43.3 7.2 %collective-permute-start.1 = (f32[27,64,128]{2,1,0:T(8,128)S(1)}, f32[27,64,128]{2,1,0:T(8,128)S(1)}, u32[]{:S(2)}, u32[]{:S(2)}) collective-permute-start(f32[27,64,128]{2,1,0:T(8,128)S(1)} %shard_map.88.refs_3_), channel_id=1, source_target_pairs={{0,384},{4,388},{8,392},{12,396},{16,400},{20,404},{24,408},{28,41... | collective-permute-start | bytes 2654216 | tf_op jit(solution)/shard_map/ppermute | solution.py:345
  50.5 2.8 %collective-permute-start.2 = (f32[27,64,128]{2,1,0:T(8,128)S(1)}, f32[27,64,128]{2,1,0:T(8,128)S(1)}, u32[]{:S(2)}, u32[]{:S(2)}) collective-permute-start(f32[27,64,128]{2,1,0:T(8,128)S(1)} %shard_map.88.refs_3_), channel_id=1, source_target_pairs={{0,256},{4,260},{8,264},{12,268},{16,272},{20,276},{24,280},{28,28... | collective-permute-start | bytes 2654216 | tf_op jit(solution)/shard_map/ppermute | solution.py:345
  53.3 2.8 %collective-permute-start.3 = (f32[27,64,128]{2,1,0:T(8,128)S(1)}, f32[27,64,128]{2,1,0:T(8,128)}, u32[]{:S(2)}, u32[]{:S(2)}) collective-permute-start(f32[27,64,128]{2,1,0:T(8,128)S(1)} %shard_map.88.refs_3_), channel_id=1, source_target_pairs={{0,128},{4,132},{8,136},{12,140},{16,144},{20,148},{24,152},{28,15... | collective-permute-start | bytes 2654216 | tf_op jit(solution)/shard_map/ppermute | solution.py:345
  56.0 8.5 %all-to-all-start = ((f32[64,4,128]{2,1,0:T(4,128)}), f32[64,4,128]{2,1,0:T(4,128)S(1)}, u32[]{:S(2)}, u32[]{:S(2)}) async-start(f32[64,4,128]{2,1,0:T(4,128)} %bitcast.1), calls=%async_computation | async-start | bytes 262144 | tf_op jit(solution)/shard_map/all_to_all | solution.py:389
  64.5 11.8 %all-gather.1 = f32[1024,128]{1,0:T(8,128)} all-gather(f32[256,128]{1,0:T(8,128)S(1)} %get-tuple-element.30), channel_id=3, replica_groups=mesh['space'=128,'chan'=4] {'chan'}, dimensions={0}, use_global_device_ids=true | all-gather | bytes 655360 | tf_op jit(solution)/shard_map/all_gather | solution.py:385
  76.3 19.6 %all-to-all-done = f32[64,4,128]{2,1,0:T(4,128)S(1)} async-done(((f32[64,4,128]{2,1,0:T(4,128)}), f32[64,4,128]{2,1,0:T(4,128)S(1)}, u32[]{:S(2)}, u32[]{:S(2)}) %all-to-all-start) | async-done | bytes 131104 | tf_op jit(solution)/shard_map/all_to_all | solution.py:389
  95.9 0.9 copy-done.4
  96.9 0.3 copy-done.5
  97.2 9.7 %shard_map.89 = (f32[256,128]{1,0:T(8,128)}, f32[128,128]{1,0:T(8,128)}, f32[256,128]{1,0:T(8,128)}, f32[256,128]{1,0:T(8,128)}, f32[256,128]{1,0:T(8,128)}, /*index=5*/f32[256,128]{1,0:T(8,128)}) custom-call(f32[656,128]{1,0:T(8,128)} %copy-done.1, f32[256,128]{1,0:T(8,128)} %bitcast.18, f32[4,256,128]{2,1,0:T(8,128)} %bitcast.16, f32[27,64,128]{2,1,0:T(8,128)} %copy-done, ...), custom_call_target="tpu_custom_call" | custom-call | tf_op jit(solution)/shard_map/pallas_call | solution.py:315
  106.9 7.6 %all-to-all-start.1 = ((f32[64,4,128]{2,1,0:T(4,128)}), f32[64,4,128]{2,1,0:T(4,128)S(1)}, u32[]{:S(2)}, u32[]{:S(2)}) async-start(f32[64,4,128]{2,1,0:T(4,128)} %bitcast.19), calls=%async_computation.1 | async-start | bytes 262144 | tf_op jit(solution)/shard_map/all_to_all | solution.py:389
  114.6 3.6 %collective-permute-start.4 = (f32[256,128]{1,0:T(8,128)}, f32[256,128]{1,0:T(8,128)S(1)}, u32[]{:S(2)}, u32[]{:S(2)}) collective-permute-start(f32[256,128]{1,0:T(8,128)} %get-tuple-element.36), channel_id=1, source_target_pairs={{0,2},{1,3},{2,0},{3,1},{4,6},{5,7},{6,4},{7,5},{8,10},{9,11},{10,... | collective-permute-start | bytes 393224 | tf_op jit(solution)/shard_map/ppermute | solution.py:348
  118.2 3.9 %collective-permute-start.5 = (f32[256,128]{1,0:T(8,128)}, f32[256,128]{1,0:T(8,128)S(1)}, u32[]{:S(2)}, u32[]{:S(2)}) collective-permute-start(f32[256,128]{1,0:T(8,128)} %get-tuple-element.37), channel_id=1, source_target_pairs={{0,3},{1,0},{2,1},{3,2},{4,7},{5,4},{6,5},{7,6},{8,11},{9,8},{10,9... | collective-permute-start | bytes 393224 | tf_op jit(solution)/shard_map/ppermute | solution.py:348
  122.1 1.9 %collective-permute-start.6 = (f32[256,128]{1,0:T(8,128)}, f32[256,128]{1,0:T(8,128)S(1)}, u32[]{:S(2)}, u32[]{:S(2)}) collective-permute-start(f32[256,128]{1,0:T(8,128)} %get-tuple-element.38), channel_id=1, source_target_pairs={{0,1},{1,2},{2,3},{3,0},{4,5},{5,6},{6,7},{7,4},{8,9},{9,10},{10,1... | collective-permute-start | bytes 393224 | tf_op jit(solution)/shard_map/ppermute | solution.py:348
  124.1 2.1 %collective-permute-done.5.refs_2_ = f32[256,128]{1,0:T(8,128)S(1)} collective-permute-done((f32[256,128]{1,0:T(8,128)}, f32[256,128]{1,0:T(8,128)S(1)}, u32[]{:S(2)}, u32[]{:S(2)}) %collective-permute-start.5) | collective-permute-done | bytes 131104 | tf_op jit(solution)/shard_map/ppermute | solution.py:348
  126.2 3.4 %collective-permute-done.6.refs_3_ = f32[256,128]{1,0:T(8,128)S(1)} collective-permute-done((f32[256,128]{1,0:T(8,128)}, f32[256,128]{1,0:T(8,128)S(1)}, u32[]{:S(2)}, u32[]{:S(2)}) %collective-permute-start.6) | collective-permute-done | bytes 131104 | tf_op jit(solution)/shard_map/ppermute | solution.py:348
  129.5 0.9 shard_map.90
  130.4 3.8 %all-gather.2 = f32[512,128]{1,0:T(8,128)S(1)} all-gather(f32[256,128]{1,0:T(8,128)S(1)} %get-tuple-element.40), channel_id=4, replica_groups={{0,4},{8,12},{16,20},{24,28},{32,36},{40,44},{48,52},{56,60},{64,68},{7..., dimensions={0}, use_global_device_ids=true | all-gather | bytes 393216 | tf_op jit(solution)/shard_map/all_gather | solution.py:351
  134.3 0.7 fusion
  (18 shorter events, 0.0 us)
Async XLA Ops:
  0.6 13.8 %collective-permute-start = (f32[27,4,128]{2,1,0:T(4,128)}, f32[27,4,128]{2,1,0:T(4,128)S(1)}, u32[]{:S(2)}, u32[]{:S(2)}) collective-permute-start(f32[27,4,128]{2,1,0:T(4,128)} %param.8), channel_id=1, source_target_pairs={{0,0},{1,128},{2,256},{3,384},{4,4},{5,132},{6,260},{7,388},{8,8},... | collective-permute-start | bytes 165896 | tf_op jit(solution)/shard_map/ppermute | solution.py:353
  13.3 1.1 copy-start.1
  43.2 53.9 %copy-start = (f32[27,64,128]{2,1,0:T(8,128)}, f32[27,64,128]{2,1,0:T(8,128)S(1)}, u32[]{:S(2)}) copy-start(f32[27,64,128]{2,1,0:T(8,128)S(1)} %shard_map.88.refs_3_) | copy-start | bytes 2654212
  43.3 52.7 %collective-permute-start.1 = (f32[27,64,128]{2,1,0:T(8,128)S(1)}, f32[27,64,128]{2,1,0:T(8,128)S(1)}, u32[]{:S(2)}, u32[]{:S(2)}) collective-permute-start(f32[27,64,128]{2,1,0:T(8,128)S(1)} %shard_map.88.refs_3_), channel_id=1, source_target_pairs={{0,384},{4,388},{8,392},{12,396},{16,400},{20,404},{24,408},{28,41... | collective-permute-start | bytes 2654216 | tf_op jit(solution)/shard_map/ppermute | solution.py:345
  50.5 45.4 %collective-permute-start.2 = (f32[27,64,128]{2,1,0:T(8,128)S(1)}, f32[27,64,128]{2,1,0:T(8,128)S(1)}, u32[]{:S(2)}, u32[]{:S(2)}) collective-permute-start(f32[27,64,128]{2,1,0:T(8,128)S(1)} %shard_map.88.refs_3_), channel_id=1, source_target_pairs={{0,256},{4,260},{8,264},{12,268},{16,272},{20,276},{24,280},{28,28... | collective-permute-start | bytes 2654216 | tf_op jit(solution)/shard_map/ppermute | solution.py:345
  53.3 42.7 %collective-permute-start.3 = (f32[27,64,128]{2,1,0:T(8,128)S(1)}, f32[27,64,128]{2,1,0:T(8,128)}, u32[]{:S(2)}, u32[]{:S(2)}) collective-permute-start(f32[27,64,128]{2,1,0:T(8,128)S(1)} %shard_map.88.refs_3_), channel_id=1, source_target_pairs={{0,128},{4,132},{8,136},{12,140},{16,144},{20,148},{24,152},{28,15... | collective-permute-start | bytes 2654216 | tf_op jit(solution)/shard_map/ppermute | solution.py:345
  56.0 39.9 %all-to-all-start = ((f32[64,4,128]{2,1,0:T(4,128)}), f32[64,4,128]{2,1,0:T(4,128)S(1)}, u32[]{:S(2)}, u32[]{:S(2)}) async-start(f32[64,4,128]{2,1,0:T(4,128)} %bitcast.1), calls=%async_computation | async-start | bytes 262144 | tf_op jit(solution)/shard_map/all_to_all | solution.py:389
  95.9 0.9 copy-start.6
  95.9 0.9 copy-start.4
  95.9 1.3 copy-start.5
  106.9 22.6 %copy-start.2 = (f32[256,128]{1,0:T(8,128)S(1)}, f32[256,128]{1,0:T(8,128)}, u32[]{:S(2)}) copy-start(f32[256,128]{1,0:T(8,128)} %get-tuple-element.35.refs_0_) | copy-start | bytes 393220
  106.9 22.6 %copy-start.3 = (f32[128,128]{1,0:T(8,128)S(1)}, f32[128,128]{1,0:T(8,128)}, u32[]{:S(2)}) copy-start(f32[128,128]{1,0:T(8,128)} %get-tuple-element.32.local_ref) | copy-start | bytes 196612
  106.9 22.6 %all-to-all-start.1 = ((f32[64,4,128]{2,1,0:T(4,128)}), f32[64,4,128]{2,1,0:T(4,128)S(1)}, u32[]{:S(2)}, u32[]{:S(2)}) async-start(f32[64,4,128]{2,1,0:T(4,128)} %bitcast.19), calls=%async_computation.1 | async-start | bytes 262144 | tf_op jit(solution)/shard_map/all_to_all | solution.py:389
  114.6 9.5 %collective-permute-start.4 = (f32[256,128]{1,0:T(8,128)}, f32[256,128]{1,0:T(8,128)S(1)}, u32[]{:S(2)}, u32[]{:S(2)}) collective-permute-start(f32[256,128]{1,0:T(8,128)} %get-tuple-element.36), channel_id=1, source_target_pairs={{0,2},{1,3},{2,0},{3,1},{4,6},{5,7},{6,4},{7,5},{8,10},{9,11},{10,... | collective-permute-start | bytes 393224 | tf_op jit(solution)/shard_map/ppermute | solution.py:348
  118.2 8.0 %collective-permute-start.5 = (f32[256,128]{1,0:T(8,128)}, f32[256,128]{1,0:T(8,128)S(1)}, u32[]{:S(2)}, u32[]{:S(2)}) collective-permute-start(f32[256,128]{1,0:T(8,128)} %get-tuple-element.37), channel_id=1, source_target_pairs={{0,3},{1,0},{2,1},{3,2},{4,7},{5,4},{6,5},{7,6},{8,11},{9,8},{10,9... | collective-permute-start | bytes 393224 | tf_op jit(solution)/shard_map/ppermute | solution.py:348
  122.1 7.4 %collective-permute-start.6 = (f32[256,128]{1,0:T(8,128)}, f32[256,128]{1,0:T(8,128)S(1)}, u32[]{:S(2)}, u32[]{:S(2)}) collective-permute-start(f32[256,128]{1,0:T(8,128)} %get-tuple-element.38), channel_id=1, source_target_pairs={{0,1},{1,2},{2,3},{3,0},{4,5},{5,6},{6,7},{7,4},{8,9},{9,10},{10,1... | collective-permute-start | bytes 393224 | tf_op jit(solution)/shard_map/ppermute | solution.py:348
